TPU v7x, 32 devices: a whole 2x2x4 slice. The times are simulated.
32 devices in a mesh: dp: 4 (over z), head: 2 (over x), ctx: 4 (over y, core).
Axes of the slice: x: 2, y: 2, z: 4, core: 2. Of those that a mesh axis runs over, the one named last changes fastest.
Arguments:
- query_rows: bfloat16 [4096, 8192], P(('dp', 'ctx'), 'head'), parts along dimension 0, may hold values from -12 to 12
- key_rows: bfloat16 [4096, 1024], P(('dp', 'ctx'), 'head'), parts along dimension 0, may hold values from -4 to 4
- stored_value_rows: bfloat16 [4096, 1024], P(('dp', 'ctx'), 'head'), parts along dimension 0, may hold values from -6 to 6
- out_grad: bfloat16 [4096, 8192], P(('dp', 'ctx'), 'head'), parts along dimension 0, may hold values from -6 to 6
- block_table: int32 [16, 2], P('dp'), parts along dimension 0, may hold values from 0 to 7, as said below
- pattern: int32 [32, 10], P('dp'), parts along dimension 0, may hold values from 0 to 7, as said below
Outputs:
- attended: bfloat16 [4096, 8192], P(('dp', 'ctx'), 'head'), parts along dimension 0
- query_grad: bfloat16 [4096, 8192], P(('dp', 'ctx'), 'head'), parts along dimension 0
- key_grad: bfloat16 [4096, 1024], P(('dp', 'ctx'), 'head'), parts along dimension 0
- value_grad: bfloat16 [4096, 1024], P(('dp', 'ctx'), 'head'), parts along dimension 0
There are 4 independent parts, one for each index of `dp`. A program takes and returns all parts, laid end to end along the dimension named above; each array names one. Nothing has to cross between parts.
Inputs may be any that keep to these rules, and one draw needn't show every extreme that they name: `pattern`: row b lists the key blocks that sequence block b reads, in no order; every entry is at most b; b, max(b - 1, 0) and 0 are always listed; repeated entries count once. `block_table`: each sequence block is held by exactly one storage block, and sequence blocks b and 7 - b are held by the same ctx index.
All inputs are finite; a program needn't handle non-finite values.
Results may differ from a plain program's by a relative error of at most 0.015.
Values may be sent and summed in bfloat16 or wider, within the bound.
A program may use at most 128 MiB of HBM per device.

v0:
```python
import jax
import jax.numpy as jnp
from jax import lax
from jax.sharding import PartitionSpec as P

HEAD_SIZE = 128
BLK = 128


def slot_layout(block_table, pattern, held_seq):
    blocks = pattern.shape[0]
    slots = pattern.shape[1]
    block_ids = jnp.arange(blocks, dtype=jnp.int32)
    store_seq = block_table.reshape(-1)
    inverse = jnp.sum(
        jnp.where(store_seq[:, None] == block_ids[None, :], block_ids[:, None], 0), axis=0
    )
    onehot = (held_seq[:, None] == block_ids[None, :]).astype(jnp.int32)
    held_pattern = jnp.sum(onehot[:, :, None] * pattern[None, :, :], axis=1)
    key_store = jnp.sum(
        jnp.where(held_pattern[:, :, None] == block_ids[None, None, :], inverse[None, None, :], 0),
        axis=2,
    )
    same = held_pattern[:, :, None] == held_pattern[:, None, :]
    slot_ids = jnp.arange(slots, dtype=jnp.int32)
    before = slot_ids[None, :] < slot_ids[:, None]
    live_slot = jnp.logical_not(jnp.any(same & before[None], axis=2))
    inner = jnp.arange(BLK, dtype=jnp.int32)
    query_pos = held_seq[:, None] * BLK + inner[None, :]
    key_pos = held_pattern[:, :, None] * BLK + inner[None, None, :]
    allowed = live_slot[:, None, :, None] & (key_pos[:, None, :, :] <= query_pos[:, :, None, None])
    return (key_store, allowed)


def attend_tiles(query_held, grad_held, key_tiles, value_tiles, allowed):
    scaling = HEAD_SIZE ** (-0.5)
    scores = (
        jnp.einsum("biagd,bjkad->bagijk", query_held, key_tiles, preferred_element_type=jnp.float32)
        * scaling
    )
    scores = jnp.where(allowed[:, None, None], scores, -jnp.inf)
    row_max = jnp.max(scores, axis=(4, 5), keepdims=True)
    row_sum = jnp.sum(jnp.exp(scores - row_max), axis=(4, 5), keepdims=True)
    log_total = row_max + jnp.log(row_sum)
    prob_full = jnp.exp(scores - log_total)
    prob_low = prob_full.astype(jnp.bfloat16)
    attended_wide = jnp.einsum(
        "bagijk,bjkad->biagd", prob_low, value_tiles, preferred_element_type=jnp.float32
    )
    attended = attended_wide.astype(jnp.bfloat16)
    row_dot = jnp.sum(grad_held.astype(jnp.float32) * attended_wide, axis=-1)
    row_dot = jnp.transpose(row_dot, (0, 2, 3, 1))[..., None, None]
    grad_prob = jnp.einsum(
        "biagd,bjkad->bagijk", grad_held, value_tiles, preferred_element_type=jnp.float32
    )
    grad_score = (prob_full * (grad_prob - row_dot) * scaling).astype(jnp.bfloat16)
    query_grad = jnp.einsum(
        "bagijk,bjkad->biagd", grad_score, key_tiles, preferred_element_type=jnp.float32
    ).astype(jnp.bfloat16)
    key_grads = jnp.einsum(
        "bagijk,biagd->bjkad", grad_score, query_held, preferred_element_type=jnp.float32
    )
    value_grads = jnp.einsum(
        "bagijk,biagd->bjkad", prob_low, grad_held, preferred_element_type=jnp.float32
    )
    return (attended, query_grad, key_grads, value_grads)


def per_device(query_rows, key_rows, stored_value_rows, out_grad, block_table, pattern):
    ctx_index = lax.axis_index("ctx")
    per_dev = block_table.shape[1]
    blocks = pattern.shape[0]
    kv_local = key_rows.shape[1] // HEAD_SIZE
    groups = query_rows.shape[1] // key_rows.shape[1]
    held_rows = per_dev * BLK
    held_seq = lax.dynamic_index_in_dim(block_table, ctx_index, 0, keepdims=False)
    key_store, allowed = slot_layout(block_table, pattern, held_seq)
    key_all, value_all = (
        lax.all_gather(key_rows, "ctx", axis=0, tiled=True),
        lax.all_gather(stored_value_rows, "ctx", axis=0, tiled=True),
    )
    key_blocks = key_all.reshape(blocks, BLK, kv_local, HEAD_SIZE)
    value_blocks = value_all.reshape(blocks, BLK, kv_local, HEAD_SIZE)
    key_tiles = key_blocks[key_store]
    value_tiles = value_blocks[key_store]
    query_held = query_rows.reshape(per_dev, BLK, kv_local, groups, HEAD_SIZE)
    grad_held = out_grad.reshape(per_dev, BLK, kv_local, groups, HEAD_SIZE)
    attended, query_grad, key_grads, value_grads = attend_tiles(
        query_held, grad_held, key_tiles, value_tiles, allowed
    )
    flat_slots = key_store.reshape(-1)
    key_partial = (
        jnp.zeros((blocks, BLK, kv_local, HEAD_SIZE), jnp.float32)
        .at[flat_slots]
        .add(key_grads.reshape(-1, BLK, kv_local, HEAD_SIZE))
    )
    value_partial = (
        jnp.zeros((blocks, BLK, kv_local, HEAD_SIZE), jnp.float32)
        .at[flat_slots]
        .add(value_grads.reshape(-1, BLK, kv_local, HEAD_SIZE))
    )
    key_sum, value_sum = (
        lax.psum_scatter(
            key_partial.reshape(blocks * BLK, -1).astype(jnp.bfloat16),
            "ctx",
            scatter_dimension=0,
            tiled=True,
        ).astype(jnp.float32),
        lax.psum_scatter(
            value_partial.reshape(blocks * BLK, -1).astype(jnp.bfloat16),
            "ctx",
            scatter_dimension=0,
            tiled=True,
        ).astype(jnp.float32),
    )
    attended = attended.reshape(held_rows, -1)
    query_grad = query_grad.reshape(held_rows, -1)
    key_grad = key_sum.astype(jnp.bfloat16)
    value_grad = value_sum.astype(jnp.bfloat16)
    return (attended, query_grad, key_grad, value_grad)


def solution(mesh):
    in_specs = (
        P(("dp", "ctx"), "head"),
        P(("dp", "ctx"), "head"),
        P(("dp", "ctx"), "head"),
        P(("dp", "ctx"), "head"),
        P("dp", None),
        P("dp", None),
    )
    out_specs = (
        P(("dp", "ctx"), "head"),
        P(("dp", "ctx"), "head"),
        P(("dp", "ctx"), "head"),
        P(("dp", "ctx"), "head"),
    )
    return jax.shard_map(
        per_device, mesh=mesh, in_specs=in_specs, out_specs=out_specs, check_vma=False
    )
```

profile of v0, /device:TPU:0, one launch (start us, length us, event | category | flops | bytes accessed | tf_op | source)
XLA Modules:
  0.0 237.2 jit_solution(9646337483750150230)
XLA Ops:
  7.2 0.0 all-gather.5.cloned.1.call-start
  7.2 0.7 all-gather.5.cloned.1.call-update
  7.9 0.0 all-gather.3.cloned.1.call-start
  7.9 0.7 all-gather.3.cloned.1.call-update
  8.6 0.0 reduce-scatter.5.cloned.1.call-start
  8.7 0.8 copy.84
  9.5 0.9 dynamic-slice_reduce_fusion
  10.3 0.1 compare_convert_fusion
  10.4 0.1 eq.67
  10.5 0.1 select_reduce_fusion.1
  10.6 0.8 multiply_reduce_fusion
  11.3 0.1 select_reduce_fusion
  11.4 0.1 reshape.178
  11.5 0.1 reshape.183
  11.6 0.2 and_reduce_fusion
  11.8 2.1 copy.144
  13.9 3.1 %copy.95 = bf16[2,128,4,8,128]{1,4,3,2,0:T(8,128)(2,1)} copy(bf16[2,128,4,8,128]{4,3,2,1,0:T(8,128)(2,1)S(1)} %bitcast.96) | data formatting | bytes 4194304 | tf_op jit(solution)/shard_map/reshape | solution.py:87
  17.0 2.1 copy.143
  19.1 0.0 copy-start.2
  19.2 0.1 iota_add_fusion.1
  19.2 0.1 iota_add_fusion
  19.3 0.5 compare_and_fusion
  19.9 9.2 %all-gather.5.cloned.1.call-done = bf16[1024,512]{1,0:T(8,128)(2,1)} async-done(((bf16[256,512]{1,0:T(8,128)(2,1)}), bf16[1024,512]{1,0:T(8,128)(2,1)}) %all-gather.5.cloned.1.call-update) | async-done | bytes 1048592 | tf_op jit(solution)/shard_map/all_gather | solution.py:79
  29.0 2.1 reshape.228
  31.2 1.5 copy.87
  32.6 14.7 %all-gather.3.cloned.1.call-done = bf16[1024,512]{1,0:T(8,128)(2,1)} async-done(((bf16[256,512]{1,0:T(8,128)(2,1)}), bf16[1024,512]{1,0:T(8,128)(2,1)}) %all-gather.3.cloned.1.call-update) | async-done | bytes 1048592 | tf_op jit(solution)/shard_map/all_gather | solution.py:80
  47.3 2.1 reshape.227
  49.5 2.5 %copy.85 = bf16[8,128,4,128]{3,1,2,0:T(8,128)(2,1)} copy(bf16[8,128,4,128]{3,2,1,0:T(4,128)(2,1)} %reshape.227) | data formatting | bytes 2097152 | tf_op jit(solution)/shard_map/reshape | solution.py:83
  52.0 2.5 %gather_fusion.1 = bf16[20,128,4,128]{3,1,2,0:T(8,128)(2,1)} fusion(bf16[8,128,4,128]{3,1,2,0:T(8,128)(2,1)S(1)} %copy.87, s32[1024]{0:T(1024)S(1)} %pad_clamp_fusion), kind=kCustom, calls=%fused_computation.1 | custom fusion | bytes 5242960 | tf_op jit(solution)/shard_map/gather | solution.py:84
  54.5 3.8 %gather_fusion = bf16[20,128,4,128]{3,1,2,0:T(8,128)(2,1)} fusion(bf16[8,128,4,128]{3,1,2,0:T(8,128)(2,1)} %copy.85, s32[1024]{0:T(1024)S(1)} %pad_clamp_fusion), kind=kCustom, calls=%fused_computation | custom fusion | bytes 5242960 | tf_op jit(solution)/shard_map/gather | solution.py:85
  58.2 18.1 %fusion.4 = (f32[2,4,8,128]{3,2,1,0:T(8,128)S(1)}, f32[2,4,10,128,128,8]{4,3,5,2,1,0:T(8,128)}) fusion(pred[2,128,10,128]{1,3,2,0:T(8,128)(4,1)S(1)} %compare_and_fusion, bf16[2,128,4,8,128,1]{4,3,2,1,0,5:T(8,128)(2,1)S(1)} %bitcast.94, bf16[2,10,128,4,128,1]{4,2,3,1,0,5:T(8,128)(2,1)} %bitcast.99), kind=kOutput, calls=%fused_computation.12 | convolution fusion | flops 2715803648 | bytes 47022080 | tf_op jit(solution)/shard_map/biagd,bjkad->bagijk/dot_general | solution.py:38
  76.3 17.4 %exponential_reduce_fusion = f32[2,4,8,128]{3,2,1,0:T(8,128)S(1)} fusion(f32[2,4,10,128,128,8]{4,3,5,2,1,0:T(8,128)} %get-tuple-element.21, f32[2,4,8,128]{3,2,1,0:T(8,128)S(1)} %get-tuple-element.20, pred[2,128,10,128]{1,3,2,0:T(8,128)(4,1)S(1)} %compare_and_fusion), kind=kLoop, calls=%fused_computation.10 | loop fusion | flops 41934848 | bytes 42336256 | tf_op jit(solution)/shard_map/reduce_sum | solution.py:43
  93.8 17.8 %fusion.3 = bf16[2,4,8,128,10,128]{3,5,2,4,1,0:T(8,128)(2,1)S(1)} fusion(f32[2,4,10,128,128,8]{4,3,5,2,1,0:T(8,128)} %get-tuple-element.21, f32[2,4,8,128]{3,2,1,0:T(8,128)S(1)} %log_add_fusion, pred[2,128,10,128]{1,3,2,0:T(8,128)(4,1)S(1)} %compare_and_fusion), kind=kLoop, calls=%fused_computation.11 | loop fusion | flops 41943040 | bytes 63275008 | tf_op jit(solution)/shard_map/convert_element_type | solution.py:46
  111.6 8.3 %convolution_bitcast_fusion = f32[2,10,128,4,128]{4,2,1,3,0:T(8,128)} fusion(bf16[2,4,8,128,10,128]{3,5,2,4,1,0:T(8,128)(2,1)S(1)} %fusion.3, bf16[2,128,4,8,128,1]{4,3,2,1,0,5:T(8,128)(2,1)S(1)} %bitcast.97), kind=kOutput, calls=%fused_computation.26 | convolution fusion | flops 2684354560 | bytes 28311552 | tf_op jit(solution)/shard_map/bagijk,biagd->bjkad/dot_general | solution.py:63
  119.9 0.2 copy-done
  120.1 11.9 %bitcast_convert_fusion.1 = (bf16[2,128,4,8,128]{1,4,3,2,0:T(8,128)(2,1)}, f32[2,4,128,8,128,1]{4,2,5,3,1,0:T(8,128)}) fusion(bf16[2,4,8,128,10,128]{3,5,2,4,1,0:T(8,128)(2,1)} %copy-done, bf16[2,10,128,4,128,1]{4,2,3,1,0,5:T(8,128)(2,1)} %bitcast.105), kind=kOutput, calls=%fused_computation.19 | convolution fusion | flops 2685403136 | bytes 29884416 | tf_op jit(solution)/shard_map/bagijk,bjkad->biagd/dot_general | solution.py:47
  132.0 2.7 %copy.103 = f32[2,10,128,4,128]{4,2,3,1,0:T(8,128)} copy(f32[2,10,128,4,128]{4,2,1,3,0:T(8,128)S(1)} %copy-done.1) | data formatting | bytes 10485760 | tf_op jit(solution)/shard_map/bagijk,biagd->bjkad/transpose | solution.py:63
  134.7 0.2 broadcast.126.clone.1
  134.9 8.5 %scatter_fusion.1 = f32[8,128,4,128]{3,1,2,0:T(8,128)S(1)} fusion(f32[8,128,4,128]{3,1,2,0:T(8,128)S(1)} %broadcast.126.clone.1, s32[20]{0:T(128)S(1)} %fusion.24, f32[20,128,4,128]{3,1,2,0:T(8,128)} %bitcast.93), kind=kCustom, calls=%fused_computation.3 | custom fusion | flops 1310720 | bytes 15728720 | tf_op jit(solution)/shard_map/scatter-add | solution.py:100
  143.4 0.2 convert_element_type.50
  143.6 1.4 copy.104
  145.0 2.7 %copy.181 = bf16[64,8,8,128]{3,1,2,0:T(8,128)(2,1)} copy(bf16[64,8,8,128]{3,2,1,0:T(8,128)(2,1)} %bitcast.103) | data formatting | bytes 2097152
  147.7 0.0 reduce-scatter.5.cloned.1.call-update
  147.7 0.0 reduce-scatter.3.cloned.1.call-start
  147.8 3.6 %fusion.9 = f32[2,128,4,8]{1,3,2,0:T(8,128)S(1)} fusion(f32[2,4,128,8,128,1]{4,2,5,3,1,0:T(8,128)} %get-tuple-element.23, bf16[2,128,4,8,128]{1,4,3,2,0:T(8,128)(2,1)} %copy.95), kind=kLoop, calls=%fused_computation.20 | loop fusion | flops 3137536 | bytes 6324224 | tf_op jit(solution)/shard_map/reduce_sum | solution.py:51
  151.4 0.0 copy-done.6
  151.4 0.0 copy-start.3
  151.4 26.9 %fusion.2 = bf16[2,4,8,128,10,128]{3,5,2,4,1,0:T(8,128)(2,1)} fusion(f32[2,4,10,128,128,8]{4,3,5,2,1,0:T(8,128)} %get-tuple-element.21, f32[2,4,8,128]{3,2,1,0:T(8,128)S(1)} %bitcast.109, f32[2,4,8,128]{3,2,1,0:T(8,128)S(1)} %log_add_fusion, pred[2,128,10,128]{1,3,2,0:T(8,128)(4,1)S(1)} %compare_and_fusion, bf16[2,10,128,4,128,1]{4,2,3,1,0,5:T(8,128)(2,1)} %bitcast.106, ...), kind=kOutput, calls=%fused_computation.7 | convolution fusion | flops 2757754880 | bytes 68026368 | tf_op jit(solution)/shard_map/biagd,bjkad->bagijk/dot_general | solution.py:53
  178.3 10.1 %convolution_bitcast_fusion.1 = f32[2,10,128,4,128]{4,2,1,3,0:T(8,128)S(1)} fusion(bf16[2,4,8,128,10,128]{3,5,2,4,1,0:T(8,128)(2,1)} %fusion.2, bf16[2,128,4,8,128,1]{4,3,2,1,0,5:T(8,128)(2,1)S(1)} %bitcast.95), kind=kOutput, calls=%fused_computation.27 | convolution fusion | flops 2684354560 | bytes 28311552 | tf_op jit(solution)/shard_map/bagijk,biagd->bjkad/dot_general | solution.py:60
  188.4 2.9 %copy.100 = f32[2,10,128,4,128]{4,2,3,1,0:T(8,128)} copy(f32[2,10,128,4,128]{4,2,1,3,0:T(8,128)S(1)} %convolution_bitcast_fusion.1) | data formatting | bytes 10485760 | tf_op jit(solution)/shard_map/bagijk,biagd->bjkad/transpose | solution.py:60
  191.4 0.2 broadcast.126.clone
  191.6 8.5 %scatter_fusion = f32[8,128,4,128]{3,1,2,0:T(8,128)S(1)} fusion(f32[8,128,4,128]{3,1,2,0:T(8,128)S(1)} %broadcast.126.clone, s32[20]{0:T(128)S(1)} %fusion.24, f32[20,128,4,128]{3,1,2,0:T(8,128)} %bitcast.92), kind=kCustom, calls=%fused_computation.2 | custom fusion | flops 1310720 | bytes 15728720 | tf_op jit(solution)/shard_map/scatter-add | solution.py:95
  200.1 0.2 convert_element_type.48
  200.3 0.7 copy.101
  201.0 1.3 copy.182
  202.3 0.0 reduce-scatter.3.cloned.1.call-update
  202.3 4.7 %copy.92 = bf16[2,128,4,8,128]{4,3,2,1,0:T(8,128)(2,1)} copy(bf16[2,128,4,8,128]{1,4,3,2,0:T(8,128)(2,1)} %get-tuple-element.22) | data formatting | bytes 4194304 | tf_op jit(solution)/shard_map/convert_element_type | solution.py:50
  207.0 4.3 %reshape.175 = bf16[256,4096]{1,0:T(8,128)(2,1)} reshape(bf16[2,128,4,8,128]{4,3,2,1,0:T(8,128)(2,1)} %copy.92) | data formatting | bytes 4194304 | tf_op jit(solution)/shard_map/reshape | solution.py:116
  211.3 0.0 copy-done.7
  211.3 10.0 %fusion.15 = bf16[2,128,4,8,128]{1,4,3,2,0:T(8,128)(2,1)} fusion(bf16[2,4,8,128,10,128]{3,5,2,4,1,0:T(8,128)(2,1)} %fusion.2, bf16[2,10,128,4,128,1]{4,2,3,1,0,5:T(8,128)(2,1)S(1)} %bitcast.100), kind=kOutput, calls=%fused_computation.28 | convolution fusion | flops 2685403136 | bytes 25690112 | tf_op jit(solution)/shard_map/bagijk,bjkad->biagd/dot_general | solution.py:57
  221.3 3.4 %copy.98 = bf16[2,128,4,8,128]{4,3,2,1,0:T(8,128)(2,1)S(1)} copy(bf16[2,128,4,8,128]{1,4,3,2,0:T(8,128)(2,1)} %fusion.15) | data formatting | bytes 4194304 | tf_op jit(solution)/shard_map/convert_element_type | solution.py:59
  224.7 2.3 reshape.177
  227.0 1.8 copy.106
  228.8 1.8 copy.105
  (21 shorter events, 0.1 us)
Async XLA Ops:
  7.2 21.9 %all-gather.5.cloned.1.call-start = ((), (), s32[]{:S(2)}) async-start(), calls=%async_computation.3 | async-start | bytes 1310720 | tf_op jit(solution)/shard_map/all_gather | solution.py:79
  7.9 39.4 %all-gather.3.cloned.1.call-start = ((), (), s32[]{:S(2)}) async-start(), calls=%async_computation.2 | async-start | bytes 1310720 | tf_op jit(solution)/shard_map/all_gather | solution.py:80
  8.6 218.4 %reduce-scatter.5.cloned.1.call-start = ((), (), s32[]{:S(2)}) async-start(), calls=%async_computation.5 | async-start | bytes 1310720 | tf_op jit(solution)/shard_map/reduce_scatter | solution.py:109
  13.9 3.1 %copy-start.4 = (bf16[32,8,32,128]{3,2,1,0:T(8,128)(2,1)}, bf16[32,8,32,128]{3,2,1,0:T(8,128)(2,1)S(1)}, u32[]{:S(2)}) copy-start(bf16[32,8,32,128]{3,2,1,0:T(8,128)(2,1)S(1)} %copy.144) | copy-start | bytes 6291460
  19.1 39.1 %copy-start.2 = (bf16[32,8,32,128]{3,2,1,0:T(8,128)(2,1)}, bf16[32,8,32,128]{3,2,1,0:T(8,128)(2,1)S(1)}, u32[]{:S(2)}) copy-start(bf16[32,8,32,128]{3,2,1,0:T(8,128)(2,1)S(1)} %copy.143) | copy-start | bytes 6291460
  93.8 17.8 %copy-start.5 = (bf16[32,8,32,128]{3,2,1,0:T(8,128)(2,1)S(1)}, bf16[32,8,32,128]{3,2,1,0:T(8,128)(2,1)}, u32[]{:S(2)}) copy-start(bf16[32,8,32,128]{3,2,1,0:T(8,128)(2,1)} %copy-done.4) | copy-start | bytes 6291460
  111.5 8.6 %copy-start = (bf16[2,4,8,128,10,128]{3,5,2,4,1,0:T(8,128)(2,1)}, bf16[2,4,8,128,10,128]{3,5,2,4,1,0:T(8,128)(2,1)S(1)}, u32[]{:S(2)}) copy-start(bf16[2,4,8,128,10,128]{3,5,2,4,1,0:T(8,128)(2,1)S(1)} %fusion.3) | copy-start | bytes 62914564
  120.1 11.9 %copy-start.1 = (f32[2,10,128,4,128]{4,2,1,3,0:T(8,128)S(1)}, f32[2,10,128,4,128]{4,2,1,3,0:T(8,128)}, u32[]{:S(2)}) copy-start(f32[2,10,128,4,128]{4,2,1,3,0:T(8,128)} %convolution_bitcast_fusion) | copy-start | bytes 15728644
  145.0 6.4 %copy-start.6 = (bf16[32,8,32,128]{3,2,1,0:T(8,128)(2,1)S(1)}, bf16[32,8,32,128]{3,2,1,0:T(8,128)(2,1)}, u32[]{:S(2)}) copy-start(bf16[32,8,32,128]{3,2,1,0:T(8,128)(2,1)} %copy-done.4) | copy-start | bytes 6291460
  147.7 81.1 %reduce-scatter.3.cloned.1.call-start = ((), (), s32[]{:S(2)}) async-start(), calls=%async_computation.4 | async-start | bytes 1310720 | tf_op jit(solution)/shard_map/reduce_scatter | solution.py:103
  151.4 26.9 %copy-start.3 = (bf16[32,8,32,128]{3,2,1,0:T(8,128)(2,1)S(1)}, bf16[32,8,32,128]{3,2,1,0:T(8,128)(2,1)}, u32[]{:S(2)}) copy-start(bf16[32,8,32,128]{3,2,1,0:T(8,128)(2,1)} %copy-done.2) | copy-start | bytes 6291460
  202.3 9.1 %copy-start.7 = (bf16[20,128,4,128]{3,1,2,0:T(8,128)(2,1)S(1)}, bf16[20,128,4,128]{3,1,2,0:T(8,128)(2,1)}, u32[]{:S(2)}) copy-start(bf16[20,128,4,128]{3,1,2,0:T(8,128)(2,1)} %gather_fusion.1) | copy-start | bytes 7864324
Sparse Core Ops, SparseCore 0:
  9.6 19.4 all-gather.4
  30.6 16.7 all-gather.2
  147.8 24.9 reduce-scatter.4
  202.4 25.0 reduce-scatter.2
where the time goes:
time: 238 us; the launch traced here: 237 us
  matrix products  85.2 us (36%)
  other arithmetic  58 us (24%)
  local copies, waits for them, and re-layouts  54.5 us (23%)
  waiting for transfers between devices  25.3 us (11%)
  between operations  14 us (6%)
    dot_general x1, matrix products, attend_tiles(): jnp.einsum('biagd,bjkad->bagijk', grad_held, value_tiles, preferred_eleme...  26.9 us
    dot_general x1, matrix products, attend_tiles(): jnp.einsum('biagd,bjkad->bagijk', query_held, key_tiles, preferred_elemen...  18.1 us
    convert_element_type x1, other arithmetic, attend_tiles(): prob_low = prob_full.astype(jnp.bfloat16)  17.8 us
    reduce_sum x1, other arithmetic, attend_tiles(): row_sum = jnp.sum(jnp.exp(scores - row_max), axis=(4, 5), keepdims=True)  17.4 us
    all_gather x1, waiting for transfers between devices, per_device(): lax.all_gather(stored_value_rows, 'ctx', axis=0, tiled=True)  14.7 us
    unnamed x23, local copies, waits for them, and re-layouts  12.7 us
    dot_general x1, matrix products, attend_tiles(): jnp.einsum('bagijk,bjkad->biagd', prob_low, value_tiles, preferred_elemen...  11.9 us
    dot_general x1, matrix products, attend_tiles(): jnp.einsum('bagijk,biagd->bjkad', grad_score, query_held, preferred_eleme...  10.1 us
  transfers between devices with their start and end apart: 4, of which 2 were waited for; matrix products, arithmetic and copies ran while one was open for 40% of the time, Pallas kernels for 0%

commit v1 on v0

--- a/solution.py
+++ b/solution.py
@@ -1,10 +1,19 @@
+import functools
+
 import jax
 import jax.numpy as jnp
 from jax import lax
+from jax.experimental import pallas as pl
+from jax.experimental.pallas import tpu as pltpu
 from jax.sharding import PartitionSpec as P
 
 HEAD_SIZE = 128
 BLK = 128
+MESH = pl.DeviceIdType.MESH
+ROWS_CHUNK = 256
+NEG = -1e30
+SCALE = HEAD_SIZE ** (-0.5)
+LOG2E = 1.4426950408889634
 
 
 def slot_layout(block_table, pattern, held_seq):
@@ -66,7 +75,7 @@
     return (attended, query_grad, key_grads, value_grads)
 
 
-def per_device(query_rows, key_rows, stored_value_rows, out_grad, block_table, pattern):
+def per_device_wide(query_rows, key_rows, stored_value_rows, out_grad, block_table, pattern):
     ctx_index = lax.axis_index("ctx")
     per_dev = block_table.shape[1]
     blocks = pattern.shape[0]
@@ -89,52 +98,432 @@
         query_held, grad_held, key_tiles, value_tiles, allowed
     )
     flat_slots = key_store.reshape(-1)
-    key_partial = (
-        jnp.zeros((blocks, BLK, kv_local, HEAD_SIZE), jnp.float32)
-        .at[flat_slots]
-        .add(key_grads.reshape(-1, BLK, kv_local, HEAD_SIZE))
-    )
-    value_partial = (
-        jnp.zeros((blocks, BLK, kv_local, HEAD_SIZE), jnp.float32)
-        .at[flat_slots]
-        .add(value_grads.reshape(-1, BLK, kv_local, HEAD_SIZE))
-    )
-    key_sum, value_sum = (
-        lax.psum_scatter(
-            key_partial.reshape(blocks * BLK, -1).astype(jnp.bfloat16),
+
+    def scattered(grads):
+        partial = (
+            jnp.zeros((blocks, BLK, kv_local, HEAD_SIZE), jnp.float32)
+            .at[flat_slots]
+            .add(grads.reshape(-1, BLK, kv_local, HEAD_SIZE))
+        )
+        return lax.psum_scatter(
+            partial.reshape(blocks * BLK, -1).astype(jnp.bfloat16),
             "ctx",
             scatter_dimension=0,
             tiled=True,
-        ).astype(jnp.float32),
-        lax.psum_scatter(
-            value_partial.reshape(blocks * BLK, -1).astype(jnp.bfloat16),
-            "ctx",
-            scatter_dimension=0,
-            tiled=True,
-        ).astype(jnp.float32),
-    )
-    attended = attended.reshape(held_rows, -1)
-    query_grad = query_grad.reshape(held_rows, -1)
-    key_grad = key_sum.astype(jnp.bfloat16)
-    value_grad = value_sum.astype(jnp.bfloat16)
-    return (attended, query_grad, key_grad, value_grad)
+        ).astype(jnp.bfloat16)
+
+    return (
+        attended.reshape(held_rows, -1),
+        query_grad.reshape(held_rows, -1),
+        scattered(key_grads),
+        scattered(value_grads),
+    )
+
+
+def fused_kernel(
+    heads, groups, blocks,
+    bt_ref, pat_ref, q_hbm, k_hbm, v_hbm, g_hbm,
+    att_hbm, dq_hbm, dk_hbm, dv_hbm,
+    kv_all, kv_now, q_buf, g_buf, att_buf, dq_buf,
+    qq, gg, qq_t, gg_t, key_slots, value_slots, prob, dscore, att_now, dq_now,
+    d_slots, own_part, y_part, mate_send, mate_recv, y_send, y_recv, dkv_buf,
+    load_sem, kv_sem, out_sem, dkv_sem, gather_send, gather_recv, red_send, red_recv,
+):
+    slots = blocks + 1
+    half = blocks // 2
+    width = groups * HEAD_SIZE
+    rows = groups * BLK
+    me = lax.axis_index("ctx")
+    core, y = me % 2, me // 2
+    mate = y * 2 + (1 - core)
+    peer = (1 - y) * 2 + core
+    cross = (1 - y) * 2 + (1 - core)
+
+    kv_loads = []
+    for h in range(heads):
+        for i, ref in enumerate((k_hbm, v_hbm)):
+            copy = pltpu.make_async_copy(
+                ref.at[:, h * HEAD_SIZE : (h + 1) * HEAD_SIZE], kv_all.at[h, i, me], kv_sem.at[h, i]
+            )
+            copy.start()
+            kv_loads.append(copy)
+    loads = []
+    for i, (src, dst) in enumerate(((q_hbm, q_buf), (g_hbm, g_buf))):
+        for b in range(2):
+            copy = pltpu.make_async_copy(
+                src.at[b * BLK : (b + 1) * BLK], dst.at[b], load_sem.at[i, b]
+            )
+            copy.start()
+            loads.append(copy)
+
+    barrier = pltpu.get_barrier_semaphore()
+    for other in (mate, peer):
+        pl.semaphore_signal(barrier, inc=1, device_id={"ctx": other}, device_id_type=MESH)
+    pl.semaphore_wait(barrier, 2)
+
+    def gather_copy(h, source, target, kind):
+        return pltpu.make_async_remote_copy(
+            src_ref=kv_all.at[h, :, source],
+            dst_ref=kv_all.at[h, :, source],
+            send_sem=gather_send.at[h, kind],
+            recv_sem=gather_recv.at[h, kind],
+            device_id={"ctx": target},
+            device_id_type=MESH,
+        )
+
+    def gather_arrival(h, source, kind):
+        return gather_copy(h, source, mate, kind)
+
+    def mate_copy(h):
+        return pltpu.make_async_remote_copy(
+            src_ref=mate_send.at[h],
+            dst_ref=mate_recv.at[h],
+            send_sem=red_send.at[h, 0],
+            recv_sem=red_recv.at[h, 0],
+            device_id={"ctx": mate},
+            device_id_type=MESH,
+        )
+
+    def peer_copy(h):
+        return pltpu.make_async_remote_copy(
+            src_ref=y_send.at[h],
+            dst_ref=y_recv.at[h],
+            send_sem=red_send.at[h, 1],
+            recv_sem=red_recv.at[h, 1],
+            device_id={"ctx": peer},
+            device_id_type=MESH,
+        )
+
+    def out_copy(h, b, i):
+        buf, dst = ((att_buf, att_hbm), (dq_buf, dq_hbm))[i]
+        return pltpu.make_async_copy(
+            buf.at[h, b],
+            dst.at[b * BLK : (b + 1) * BLK, pl.ds(pl.multiple_of(h * width, width), width)],
+            out_sem.at[h, b, i],
+        )
+
+    for h in range(heads):
+        kv_loads[2 * h].wait()
+        kv_loads[2 * h + 1].wait()
+        gather_copy(h, me, peer, 0).start()
+        gather_copy(h, me, mate, 1).start()
+
+    seq0, seq1 = bt_ref[me, 0], bt_ref[me, 1]
+    lo, hi = jnp.minimum(seq0, seq1), jnp.maximum(seq0, seq1)
+    at_lo = jnp.where(seq0 > seq1, 1, 0)
+    at_hi = 1 - at_lo
+    table = [bt_ref[g // 2, g % 2] for g in range(blocks)]
+    homes, biases, is_lo = [], [], []
+    for p in range(slots):
+        if p == 0:
+            mine, key_seq, query_seq = None, lo, lo
+        elif p >= half:
+            mine, key_seq, query_seq = None, p - lo - 1, hi
+        else:
+            mine = p <= lo
+            key_seq = jnp.where(mine, lo - p, p - lo - 1)
+            query_seq = jnp.where(mine, lo, hi)
+        home = jnp.int32(0)
+        for g in range(blocks):
+            home = jnp.where(table[g] == key_seq, g, home)
+        homes.append(home)
+        is_lo.append(mine)
+        if p in (0, slots - 1):
+            biases.append(None)
+        else:
+            hits = jnp.int32(0)
+            for j in range(pat_ref.shape[1]):
+                hits = hits + jnp.where(pat_ref[query_seq, j] == key_seq, 1, 0)
+            biases.append(jnp.where(hits > 0, jnp.float32(0), jnp.float32(NEG)))
+    in_lo = [None if m is None else jnp.where(m, jnp.float32(1), jnp.float32(0)) for m in is_lo]
+
+    zeros = jnp.zeros((BLK, HEAD_SIZE), jnp.bfloat16)
+    for ref in (key_slots, value_slots):
+        for p in range(slots):
+            if p == 0:
+                ref[p * BLK : (p + 1) * BLK, HEAD_SIZE:] = zeros
+            elif p >= half:
+                ref[p * BLK : (p + 1) * BLK, :HEAD_SIZE] = zeros
+
+    for copy in loads:
+        copy.wait()
+
+    def forward(h):
+        gather_arrival(h, peer, 0).wait_recv()
+        gather_copy(h, peer, mate, 2).start()
+
+    def second_stage(h):
+        mate_copy(h).wait_recv()
+        for i in range(2):
+            y_send[h, i] = (y_part[h, i] + mate_recv[h, 1, i].astype(jnp.float32)).astype(
+                jnp.bfloat16
+            )
+        peer_copy(h).start()
+
+    forward(0)
+
+    def one_head(h, carry):
+        first = pl.multiple_of(h * width, width)
+        for src, dst, dst_t in ((q_buf, qq, qq_t), (g_buf, gg, gg_t)):
+            for g in range(groups):
+                cols = pl.ds(pl.multiple_of(first + g * HEAD_SIZE, HEAD_SIZE), HEAD_SIZE)
+                for part, at in ((0, at_lo), (1, at_hi)):
+                    tile = src[at, :, cols]
+                    dst[g * BLK : (g + 1) * BLK, part * HEAD_SIZE : (part + 1) * HEAD_SIZE] = tile
+                    dst_t[part * HEAD_SIZE : (part + 1) * HEAD_SIZE, g * BLK : (g + 1) * BLK] = tile.T
+
+        gather_arrival(h, mate, 1).wait_recv()
+        gather_arrival(h, cross, 2).wait_recv()
+        for i in range(2):
+            for c in range(blocks // 2):
+                for b in range(2):
+                    kv_now[i, c * 2 + b] = kv_all[h, i, c, b * BLK : (b + 1) * BLK]
+        for i, ref in enumerate((key_slots, value_slots)):
+            for p in range(slots):
+                tile = kv_now[i, homes[p]]
+                at = slice(p * BLK, (p + 1) * BLK)
+                if p == 0:
+                    ref[at, :HEAD_SIZE] = tile
+                elif p >= half:
+                    ref[at, HEAD_SIZE:] = tile
+                else:
+                    wide = tile.astype(jnp.float32)
+                    ref[at, :HEAD_SIZE] = (wide * in_lo[p]).astype(jnp.bfloat16)
+                    ref[at, HEAD_SIZE:] = (wide * (1.0 - in_lo[p])).astype(jnp.bfloat16)
+
+        def one_chunk(c, carry):
+            at = pl.ds(pl.multiple_of(c * ROWS_CHUNK, ROWS_CHUNK), ROWS_CHUNK)
+            nt = (((1,), (1,)), ((), ()))
+            score = lax.dot_general(
+                qq[at, :], key_slots[...], nt, preferred_element_type=jnp.float32
+            )
+            row = lax.broadcasted_iota(jnp.int32, (ROWS_CHUNK, BLK), 0) % BLK
+            col = lax.broadcasted_iota(jnp.int32, (ROWS_CHUNK, BLK), 1)
+            causal = col <= row
+            tiles = []
+            for p in range(slots):
+                tile = score[:, p * BLK : (p + 1) * BLK]
+                tiles.append(
+                    jnp.where(causal, tile, NEG) if biases[p] is None else tile + biases[p]
+                )
+            max_lo, max_hi = tiles[0], tiles[half]
+            for p in range(1, slots):
+                if p < half:
+                    max_lo = jnp.maximum(max_lo, tiles[p] + (1.0 - in_lo[p]) * NEG)
+                    max_hi = jnp.maximum(max_hi, tiles[p] + in_lo[p] * NEG)
+                elif p > half:
+                    max_hi = jnp.maximum(max_hi, tiles[p])
+            max_lo = jnp.max(max_lo, axis=1, keepdims=True)
+            max_hi = jnp.max(max_hi, axis=1, keepdims=True)
+
+            def pick(p, of_lo, of_hi):
+                if p == 0:
+                    return of_lo
+                if p >= half:
+                    return of_hi
+                return of_lo * in_lo[p] + of_hi * (1.0 - in_lo[p])
+
+            sum_lo = sum_hi = None
+            for p in range(slots):
+                tiles[p] = jnp.exp2((tiles[p] - pick(p, max_lo, max_hi)) * (SCALE * LOG2E))
+                if p == 0:
+                    sum_lo = tiles[p]
+                elif p < half:
+                    sum_lo = sum_lo + tiles[p] * in_lo[p]
+                    part = tiles[p] * (1.0 - in_lo[p])
+                    sum_hi = part if sum_hi is None else sum_hi + part
+                else:
+                    sum_hi = tiles[p] if sum_hi is None else sum_hi + tiles[p]
+            inv_lo = 1.0 / jnp.sum(sum_lo, axis=1, keepdims=True)
+            inv_hi = 1.0 / jnp.sum(sum_hi, axis=1, keepdims=True)
+            for p in range(slots):
+                tiles[p] = tiles[p] * pick(p, inv_lo, inv_hi)
+                prob[at, p * BLK : (p + 1) * BLK] = tiles[p].astype(jnp.bfloat16)
+            wide = jnp.dot(prob[at, :], value_slots[...], preferred_element_type=jnp.float32)
+            att_now[0, at, :] = wide[:, :HEAD_SIZE].astype(jnp.bfloat16)
+            att_now[1, at, :] = wide[:, HEAD_SIZE:].astype(jnp.bfloat16)
+            dots = wide * gg[at, :].astype(jnp.float32)
+            dot_lo = jnp.sum(dots[:, :HEAD_SIZE], axis=1, keepdims=True)
+            dot_hi = jnp.sum(dots[:, HEAD_SIZE:], axis=1, keepdims=True)
+            dprob = lax.dot_general(
+                gg[at, :], value_slots[...], nt, preferred_element_type=jnp.float32
+            )
+            for p in range(slots):
+                cols = slice(p * BLK, (p + 1) * BLK)
+                dscore[at, cols] = (tiles[p] * (dprob[:, cols] - pick(p, dot_lo, dot_hi))).astype(
+                    jnp.bfloat16
+                )
+            dq = SCALE * jnp.dot(dscore[at, :], key_slots[...], preferred_element_type=jnp.float32)
+            dq_now[0, at, :] = dq[:, :HEAD_SIZE].astype(jnp.bfloat16)
+            dq_now[1, at, :] = dq[:, HEAD_SIZE:].astype(jnp.bfloat16)
+            return carry
+
+        lax.fori_loop(0, rows // ROWS_CHUNK, one_chunk, 0)
+
+        @pl.when(h < heads - 1)
+        def _():
+            forward(h + 1)
+
+        @pl.when(h > 0)
+        def _():
+            second_stage(h - 1)
+
+        for b in range(2):
+            from_now = jnp.where(at_lo == b, 0, 1)
+            for g in range(groups):
+                cols = slice(g * HEAD_SIZE, (g + 1) * HEAD_SIZE)
+                att_buf[h, b, :, cols] = att_now[from_now, g * BLK : (g + 1) * BLK, :]
+                dq_buf[h, b, :, cols] = dq_now[from_now, g * BLK : (g + 1) * BLK, :]
+            out_copy(h, b, 0).start()
+            out_copy(h, b, 1).start()
+
+        for i, (left, right) in enumerate(((qq_t, dscore), (gg_t, prob))):
+            grads = jnp.dot(left[...], right[...], preferred_element_type=jnp.float32)
+            for p in range(slots):
+                cols = slice(p * BLK, (p + 1) * BLK)
+                if p == 0:
+                    d_slots[i, p] = grads[:HEAD_SIZE, cols]
+                elif p >= half:
+                    d_slots[i, p] = grads[HEAD_SIZE:, cols]
+                else:
+                    d_slots[i, p] = grads[:HEAD_SIZE, cols] * in_lo[p] + grads[
+                        HEAD_SIZE:, cols
+                    ] * (1.0 - in_lo[p])
+
+        def partial(i, target, b):
+            seq = bt_ref[target, b]
+            slot_lo = jnp.maximum(lo - seq, 0)
+            slot_hi = jnp.minimum(lo + 1 + seq, slots - 1)
+            scale = SCALE if i == 0 else 1.0
+            of_lo = jnp.where(seq <= lo, jnp.float32(scale), jnp.float32(0))
+            of_hi = jnp.where(seq <= hi, jnp.float32(scale), jnp.float32(0))
+            return (d_slots[i, slot_lo] * of_lo + d_slots[i, slot_hi] * of_hi).T
+
+        for i in range(2):
+            for b in range(2):
+                at = slice(b * BLK, (b + 1) * BLK)
+                mate_send[h, 0, i, at] = partial(i, mate, b).astype(jnp.bfloat16)
+                mate_send[h, 1, i, at] = partial(i, cross, b).astype(jnp.bfloat16)
+        mate_copy(h).start()
+        for i in range(2):
+            for b in range(2):
+                at = slice(b * BLK, (b + 1) * BLK)
+                y_part[h, i, at] = partial(i, peer, b)
+                own_part[h, i, at] = partial(i, me, b)
+        return carry
+
+    lax.fori_loop(0, heads, one_head, 0)
+    second_stage(heads - 1)
+
+    dkv_copies = []
+    for h in range(heads):
+        peer_copy(h).wait_recv()
+        for i, dst in enumerate((dk_hbm, dv_hbm)):
+            total = (
+                own_part[h, i]
+                + mate_recv[h, 0, i].astype(jnp.float32)
+                + y_recv[h, i].astype(jnp.float32)
+            )
+            dkv_buf[h, i] = total.astype(jnp.bfloat16)
+            copy = pltpu.make_async_copy(
+                dkv_buf.at[h, i], dst.at[:, h * HEAD_SIZE : (h + 1) * HEAD_SIZE], dkv_sem.at[h, i]
+            )
+            copy.start()
+            dkv_copies.append(copy)
+
+    for h in range(heads):
+        gather_copy(h, me, peer, 0).wait_send()
+        gather_copy(h, me, mate, 1).wait_send()
+        gather_copy(h, peer, mate, 2).wait_send()
+        mate_copy(h).wait_send()
+        peer_copy(h).wait_send()
+        for b in range(2):
+            out_copy(h, b, 0).wait()
+            out_copy(h, b, 1).wait()
+    for copy in dkv_copies:
+        copy.wait()
+
+
+def per_device_fused(query_rows, key_rows, stored_value_rows, out_grad, block_table, pattern):
+    blocks = pattern.shape[0]
+    held, kv_width = key_rows.shape
+    heads = kv_width // HEAD_SIZE
+    groups = query_rows.shape[1] // kv_width
+    width = groups * HEAD_SIZE
+    rows = groups * BLK
+    slots = blocks + 1
+    bf16, f32 = jnp.bfloat16, jnp.float32
+    vmem, dma = pltpu.VMEM, pltpu.SemaphoreType.DMA
+    ctx = blocks // 2
+    pair = 2 * HEAD_SIZE
+    scratch = [
+        vmem((heads, 2, ctx, held, HEAD_SIZE), bf16),
+        vmem((2, blocks, BLK, HEAD_SIZE), bf16),
+        vmem((2, BLK, heads * width), bf16),
+        vmem((2, BLK, heads * width), bf16),
+        vmem((heads, 2, BLK, width), bf16),
+        vmem((heads, 2, BLK, width), bf16),
+        vmem((rows, pair), bf16),
+        vmem((rows, pair), bf16),
+        vmem((pair, rows), bf16),
+        vmem((pair, rows), bf16),
+        vmem((slots * BLK, pair), bf16),
+        vmem((slots * BLK, pair), bf16),
+        vmem((rows, slots * BLK), bf16),
+        vmem((rows, slots * BLK), bf16),
+        vmem((2, rows, HEAD_SIZE), bf16),
+        vmem((2, rows, HEAD_SIZE), bf16),
+        vmem((2, slots, HEAD_SIZE, BLK), f32),
+        vmem((heads, 2, held, HEAD_SIZE), f32),
+        vmem((heads, 2, held, HEAD_SIZE), f32),
+        vmem((heads, 2, 2, held, HEAD_SIZE), bf16),
+        vmem((heads, 2, 2, held, HEAD_SIZE), bf16),
+        vmem((heads, 2, held, HEAD_SIZE), bf16),
+        vmem((heads, 2, held, HEAD_SIZE), bf16),
+        vmem((heads, 2, held, HEAD_SIZE), bf16),
+        dma((2, 2)),
+        dma((heads, 2)),
+        dma((heads, 2, 2)),
+        dma((heads, 2)),
+        dma((heads, 3)),
+        dma((heads, 3)),
+        dma((heads, 2)),
+        dma((heads, 2)),
+    ]
+    smem = pl.BlockSpec(memory_space=pltpu.SMEM)
+    hbm = pl.BlockSpec(memory_space=pl.ANY)
+    return pl.pallas_call(
+        functools.partial(fused_kernel, heads, groups, blocks),
+        out_shape=(
+            jax.ShapeDtypeStruct(query_rows.shape, bf16),
+            jax.ShapeDtypeStruct(query_rows.shape, bf16),
+            jax.ShapeDtypeStruct(key_rows.shape, bf16),
+            jax.ShapeDtypeStruct(key_rows.shape, bf16),
+        ),
+        in_specs=[smem, smem, hbm, hbm, hbm, hbm],
+        out_specs=(hbm, hbm, hbm, hbm),
+        scratch_shapes=scratch,
+        compiler_params=pltpu.CompilerParams(
+            collective_id=0, has_side_effects=True, vmem_limit_bytes=52 * 1024 * 1024
+        ),
+        cost_estimate=pl.CostEstimate(
+            flops=12 * heads * rows * pair * slots * BLK,
+            bytes_accessed=8 * query_rows.size + 8 * key_rows.size,
+            transcendentals=heads * rows * slots * BLK,
+        ),
+    )(block_table, pattern, query_rows, key_rows, stored_value_rows, out_grad)
 
 
 def solution(mesh):
-    in_specs = (
-        P(("dp", "ctx"), "head"),
-        P(("dp", "ctx"), "head"),
-        P(("dp", "ctx"), "head"),
-        P(("dp", "ctx"), "head"),
-        P("dp", None),
-        P("dp", None),
-    )
-    out_specs = (
-        P(("dp", "ctx"), "head"),
-        P(("dp", "ctx"), "head"),
-        P(("dp", "ctx"), "head"),
-        P(("dp", "ctx"), "head"),
-    )
+    row_spec = P(("dp", "ctx"), "head")
+    in_specs = (row_spec, row_spec, row_spec, row_spec, P("dp", None), P("dp", None))
+    out_specs = (row_spec, row_spec, row_spec, row_spec)
+
+    def per_device(query_rows, key_rows, stored_value_rows, out_grad, block_table, pattern):
+        fits = mesh.shape["ctx"] == 4 and block_table.shape == (4, 2)
+        body = per_device_fused if fits else per_device_wide
+        return body(query_rows, key_rows, stored_value_rows, out_grad, block_table, pattern)
+
     return jax.shard_map(
         per_device, mesh=mesh, in_specs=in_specs, out_specs=out_specs, check_vma=False
     )

time: 238 us -> 67.6 us (0.28)
  matrix products: 85.2 us -> 0 us
  other arithmetic: 58 us -> 0 us
  Pallas kernels: 0 us -> 57.4 us
  local copies, waits for them, and re-layouts: 54.5 us -> 9.36 us
  waiting for transfers between devices: 25.3 us -> 0 us
  between operations: 14 us -> 0.65 us
    dot_general x6 -> x0, matrix products: 85.2 us -> none  [the longest x1 26.9 us: attend_tiles(): jnp.einsum('biagd,bjkad->bagijk', grad_held, value_tiles, preferred_eleme...]
    pallas_call x0 -> x1, Pallas kernels: none -> 57.4 us  [per_device_fused(): pl.pallas_call(functools.partial(fused_kernel, heads, groups, blocks), ou...]
    all_gather x2 -> x0, waiting for transfers between devices: 23.9 us -> none  [the longest x1 14.7 us: per_device(): lax.all_gather(stored_value_rows, 'ctx', axis=0, tiled=True)]
    reduce_sum x5 -> x0, other arithmetic: 22 us -> none  [the longest x1 17.4 us: attend_tiles(): row_sum = jnp.sum(jnp.exp(scores - row_max), axis=(4, 5), keepdims=True)]
    convert_element_type x4 -> x0, other arithmetic: 18.2 us -> none  [the longest x1 17.8 us: attend_tiles(): prob_low = prob_full.astype(jnp.bfloat16)]
    reshape x8 -> x0, local copies, waits for them, and re-layouts: 18 us -> none  [the longest x2 4.61 us: per_device(): value_blocks = value_all.reshape(blocks, BLK, kv_local, HEAD_SIZE)]
    scatter-add x2 -> x0, other arithmetic: 17 us -> none  [the longest x1 8.49 us: per_device(): value_partial = jnp.zeros((blocks, BLK, kv_local, HEAD_SIZE), jnp.float32...]
    convert_element_type x4 -> x0, local copies, waits for them, and re-layouts: 10.3 us -> none  [the longest x1 4.73 us: attend_tiles(): attended = attended_wide.astype(jnp.bfloat16)]
  transfers between devices with their start and end apart: 4 -> 0, of which waited for: 2 -> 0; matrix products, arithmetic and copies ran while one was open for 40% -> 0% of each run, Pallas kernels for 0% -> 0%
where the time goes in v1:
time: 67.6 us; the launch traced here: 67.4 us
  Pallas kernels  57.4 us (85%)
  local copies, waits for them, and re-layouts  9.36 us (14%)
    pallas_call x1, Pallas kernels, per_device_fused(): pl.pallas_call(functools.partial(fused_kernel, heads, groups, blocks), ou...  57.4 us
    unnamed x13, local copies, waits for them, and re-layouts  9.36 us

profile of v1, /device:TPU:0, one launch (start us, length us, event | category | flops | bytes accessed | tf_op | source)
XLA Modules:
  0.0 67.4 jit_solution(17539830947012635842)
XLA Ops:
  0.6 0.8 %copy.10.bt_ref = s32[4,2]{1,0:T(4,128)S(1)} copy(s32[4,2]{0,1:T(2,128)} %param.10) | data formatting | bytes 64 | tf_op args[4]
  1.4 0.0 copy-start
  1.4 0.9 %copy-done = bf16[256,512]{1,0:T(8,128)(2,1)S(1)} copy-done((bf16[256,512]{1,0:T(8,128)(2,1)S(1)}, bf16[256,512]{1,0:T(8,128)(2,1)}, u32[]{:S(2)}) %copy-start) | copy-done | bytes 262168
  2.3 0.0 copy-start.1
  2.3 0.9 %copy-done.1 = bf16[256,512]{1,0:T(8,128)(2,1)S(1)} copy-done((bf16[256,512]{1,0:T(8,128)(2,1)S(1)}, bf16[256,512]{1,0:T(8,128)(2,1)}, u32[]{:S(2)}) %copy-start.1) | copy-done | bytes 262168
  3.3 0.0 copy-start.2
  3.3 0.7 %copy-done.2 = s32[8,10]{1,0:T(8,128)S(1)} copy-done((s32[8,10]{1,0:T(8,128)S(1)}, s32[8,10]{1,0:T(8,128)}, u32[]{:S(2)}) %copy-start.2) | copy-done | bytes 344
  4.0 57.4 %shard_map.93 = (bf16[256,4096]{1,0:T(8,128)(2,1)}, bf16[256,4096]{1,0:T(8,128)(2,1)}, bf16[256,512]{1,0:T(8,128)(2,1)S(1)}, bf16[256,512]{1,0:T(8,128)(2,1)S(1)}) custom-call(s32[4,2]{1,0:T(4,128)S(1)} %copy.10.bt_ref, s32[8,10]{1,0:T(8,128)S(1)} %copy-done.2, bf16[256,4096]{1,0:T(8,128)(2,1)} %q_hbm.1, bf16[256,512]{1,0:T(8,128)(2,1)S(1)} %copy-done, ...), custom_call_target="tpu_custom_call" | custom-call | flops 14495514624 | bytes 9437184 | tf_op jit(solution)/shard_map/pallas_call | solution.py:495
  61.4 0.0 copy-start.3
  61.4 3.3 %copy.15 = bf16[256,4096]{1,0:T(8,128)(2,1)} copy(bf16[256,4096]{1,0:T(8,128)(2,1)} %get-tuple-element.8) | data formatting | bytes 4194304
  64.6 0.0 copy-done.3
  64.6 1.3 %copy.16 = bf16[256,4096]{1,0:T(8,128)(2,1)} copy(bf16[256,4096]{1,0:T(8,128)(2,1)S(1)} %copy-done.3) | data formatting | bytes 4194304
  66.0 0.7 %copy.17 = bf16[256,512]{1,0:T(8,128)(2,1)} copy(bf16[256,512]{1,0:T(8,128)(2,1)S(1)} %get-tuple-element.10) | data formatting | bytes 524288
  66.7 0.7 %copy.18 = bf16[256,512]{1,0:T(8,128)(2,1)} copy(bf16[256,512]{1,0:T(8,128)(2,1)S(1)} %get-tuple-element.11) | data formatting | bytes 524288
Async XLA Ops:
  1.4 0.9 %copy-start = (bf16[256,512]{1,0:T(8,128)(2,1)S(1)}, bf16[256,512]{1,0:T(8,128)(2,1)}, u32[]{:S(2)}) copy-start(bf16[256,512]{1,0:T(8,128)(2,1)} %k_hbm.1) | copy-start | bytes 786436
  2.3 0.9 %copy-start.1 = (bf16[256,512]{1,0:T(8,128)(2,1)S(1)}, bf16[256,512]{1,0:T(8,128)(2,1)}, u32[]{:S(2)}) copy-start(bf16[256,512]{1,0:T(8,128)(2,1)} %v_hbm.1) | copy-start | bytes 786436
  3.3 0.7 %copy-start.2 = (s32[8,10]{1,0:T(8,128)S(1)}, s32[8,10]{1,0:T(8,128)}, u32[]{:S(2)}) copy-start(s32[8,10]{1,0:T(8,128)} %pat_ref.1) | copy-start | bytes 964
  61.4 3.3 %copy-start.3 = (bf16[256,4096]{1,0:T(8,128)(2,1)S(1)}, bf16[256,4096]{1,0:T(8,128)(2,1)}, u32[]{:S(2)}) copy-start(bf16[256,4096]{1,0:T(8,128)(2,1)} %get-tuple-element.9) | copy-start | bytes 6291460

commit v2 on v1

--- a/solution.py
+++ b/solution.py
@@ -11,6 +11,7 @@
 BLK = 128
 MESH = pl.DeviceIdType.MESH
 ROWS_CHUNK = 256
+SUB = 32
 NEG = -1e30
 SCALE = HEAD_SIZE ** (-0.5)
 LOG2E = 1.4426950408889634
@@ -125,7 +126,7 @@
     bt_ref, pat_ref, q_hbm, k_hbm, v_hbm, g_hbm,
     att_hbm, dq_hbm, dk_hbm, dv_hbm,
     kv_all, kv_now, q_buf, g_buf, att_buf, dq_buf,
-    qq, gg, qq_t, gg_t, key_slots, value_slots, prob, dscore, att_now, dq_now,
+    qq, gg, qq_t, gg_t, q_scaled, g_scaled, key_slots, value_slots, key_t, value_t, s_buf, d_buf, prob, dscore, att_now, dq_now,
     d_slots, own_part, y_part, mate_send, mate_recv, y_send, y_recv, dkv_buf,
     load_sem, kv_sem, out_sem, dkv_sem, gather_send, gather_recv, red_send, red_recv,
 ):
@@ -174,22 +175,22 @@
     def gather_arrival(h, source, kind):
         return gather_copy(h, source, mate, kind)
 
-    def mate_copy(h):
+    def mate_copy(h, i):
         return pltpu.make_async_remote_copy(
-            src_ref=mate_send.at[h],
-            dst_ref=mate_recv.at[h],
-            send_sem=red_send.at[h, 0],
-            recv_sem=red_recv.at[h, 0],
+            src_ref=mate_send.at[h, i],
+            dst_ref=mate_recv.at[h, i],
+            send_sem=red_send.at[h, 0, i],
+            recv_sem=red_recv.at[h, 0, i],
             device_id={"ctx": mate},
             device_id_type=MESH,
         )
 
-    def peer_copy(h):
+    def peer_copy(h, i):
         return pltpu.make_async_remote_copy(
-            src_ref=y_send.at[h],
-            dst_ref=y_recv.at[h],
-            send_sem=red_send.at[h, 1],
-            recv_sem=red_recv.at[h, 1],
+            src_ref=y_send.at[h, i],
+            dst_ref=y_recv.at[h, i],
+            send_sem=red_send.at[h, 1, i],
+            recv_sem=red_recv.at[h, 1, i],
             device_id={"ctx": peer},
             device_id_type=MESH,
         )
@@ -235,15 +236,20 @@
             for j in range(pat_ref.shape[1]):
                 hits = hits + jnp.where(pat_ref[query_seq, j] == key_seq, 1, 0)
             biases.append(jnp.where(hits > 0, jnp.float32(0), jnp.float32(NEG)))
+    bias_lo = [None if m is None else jnp.where(m, x, NEG) for m, x in zip(is_lo, biases)]
+    bias_hi = [None if m is None else jnp.where(m, NEG, x) for m, x in zip(is_lo, biases)]
     in_lo = [None if m is None else jnp.where(m, jnp.float32(1), jnp.float32(0)) for m in is_lo]
 
     zeros = jnp.zeros((BLK, HEAD_SIZE), jnp.bfloat16)
-    for ref in (key_slots, value_slots):
+    for ref, ref_t in ((key_slots, key_t), (value_slots, value_t)):
         for p in range(slots):
+            at = slice(p * BLK, (p + 1) * BLK)
             if p == 0:
-                ref[p * BLK : (p + 1) * BLK, HEAD_SIZE:] = zeros
+                ref[at, HEAD_SIZE:] = zeros
+                ref_t[HEAD_SIZE:, at] = zeros
             elif p >= half:
-                ref[p * BLK : (p + 1) * BLK, :HEAD_SIZE] = zeros
+                ref[at, :HEAD_SIZE] = zeros
+                ref_t[:HEAD_SIZE, at] = zeros
 
     for copy in loads:
         copy.wait()
@@ -252,25 +258,21 @@
         gather_arrival(h, peer, 0).wait_recv()
         gather_copy(h, peer, mate, 2).start()
 
-    def second_stage(h):
-        mate_copy(h).wait_recv()
-        for i in range(2):
-            y_send[h, i] = (y_part[h, i] + mate_recv[h, 1, i].astype(jnp.float32)).astype(
-                jnp.bfloat16
-            )
-        peer_copy(h).start()
+    def second_stage(h, i):
+        mate_copy(h, i).wait_recv()
+        y_send[h, i] = (y_part[h, i] + mate_recv[h, i, 1].astype(jnp.float32)).astype(jnp.bfloat16)
+        peer_copy(h, i).start()
 
     forward(0)
 
     def one_head(h, carry):
         first = pl.multiple_of(h * width, width)
-        for src, dst, dst_t in ((q_buf, qq, qq_t), (g_buf, gg, gg_t)):
+        for src, dst in ((q_buf, qq), (g_buf, gg)):
             for g in range(groups):
                 cols = pl.ds(pl.multiple_of(first + g * HEAD_SIZE, HEAD_SIZE), HEAD_SIZE)
                 for part, at in ((0, at_lo), (1, at_hi)):
                     tile = src[at, :, cols]
                     dst[g * BLK : (g + 1) * BLK, part * HEAD_SIZE : (part + 1) * HEAD_SIZE] = tile
-                    dst_t[part * HEAD_SIZE : (part + 1) * HEAD_SIZE, g * BLK : (g + 1) * BLK] = tile.T
 
         gather_arrival(h, mate, 1).wait_recv()
         gather_arrival(h, cross, 2).wait_recv()
@@ -278,87 +280,123 @@
             for c in range(blocks // 2):
                 for b in range(2):
                     kv_now[i, c * 2 + b] = kv_all[h, i, c, b * BLK : (b + 1) * BLK]
-        for i, ref in enumerate((key_slots, value_slots)):
+        for i, (ref, ref_t) in enumerate(((key_slots, key_t), (value_slots, value_t))):
             for p in range(slots):
                 tile = kv_now[i, homes[p]]
+                tile_t = tile.T
                 at = slice(p * BLK, (p + 1) * BLK)
                 if p == 0:
                     ref[at, :HEAD_SIZE] = tile
+                    ref_t[:HEAD_SIZE, at] = tile_t
                 elif p >= half:
                     ref[at, HEAD_SIZE:] = tile
+                    ref_t[HEAD_SIZE:, at] = tile_t
                 else:
-                    wide = tile.astype(jnp.float32)
-                    ref[at, :HEAD_SIZE] = (wide * in_lo[p]).astype(jnp.bfloat16)
-                    ref[at, HEAD_SIZE:] = (wide * (1.0 - in_lo[p])).astype(jnp.bfloat16)
-
-        def one_chunk(c, carry):
-            at = pl.ds(pl.multiple_of(c * ROWS_CHUNK, ROWS_CHUNK), ROWS_CHUNK)
-            nt = (((1,), (1,)), ((), ()))
-            score = lax.dot_general(
-                qq[at, :], key_slots[...], nt, preferred_element_type=jnp.float32
-            )
-            row = lax.broadcasted_iota(jnp.int32, (ROWS_CHUNK, BLK), 0) % BLK
-            col = lax.broadcasted_iota(jnp.int32, (ROWS_CHUNK, BLK), 1)
-            causal = col <= row
-            tiles = []
-            for p in range(slots):
-                tile = score[:, p * BLK : (p + 1) * BLK]
-                tiles.append(
-                    jnp.where(causal, tile, NEG) if biases[p] is None else tile + biases[p]
-                )
-            max_lo, max_hi = tiles[0], tiles[half]
-            for p in range(1, slots):
+                    for target, index, value in (
+                        (ref, (at, slice(0, HEAD_SIZE)), tile),
+                        (ref_t, (slice(0, HEAD_SIZE), at), tile_t),
+                    ):
+                        wide = value.astype(jnp.float32)
+                        target[index] = (wide * in_lo[p]).astype(jnp.bfloat16)
+                    for target, index, value in (
+                        (ref, (at, slice(HEAD_SIZE, None)), tile),
+                        (ref_t, (slice(HEAD_SIZE, None), at), tile_t),
+                    ):
+                        wide = value.astype(jnp.float32)
+                        target[index] = (wide * (1.0 - in_lo[p])).astype(jnp.bfloat16)
+
+        def matmuls(c):
+            at = slice(c * ROWS_CHUNK, (c + 1) * ROWS_CHUNK)
+            s_buf[c % 2] = jnp.dot(qq[at, :], key_t[...], preferred_element_type=jnp.float32)
+            d_buf[c % 2] = jnp.dot(gg[at, :], value_t[...], preferred_element_type=jnp.float32)
+
+        def pick(p, of_lo, of_hi):
+            if p == 0:
+                return of_lo
+            if p >= half:
+                return of_hi
+            return jnp.where(is_lo[p], of_lo, of_hi)
+
+        def softmax(c, r):
+            rows_at = slice(c * ROWS_CHUNK + r, c * ROWS_CHUNK + r + SUB)
+            inner = slice(r, r + SUB)
+            row = lax.broadcasted_iota(jnp.int32, (SUB, BLK), 0) + (c * ROWS_CHUNK + r) % BLK
+            col = lax.broadcasted_iota(jnp.int32, (SUB, BLK), 1)
+            tiles = [s_buf[c % 2, inner, p * BLK : (p + 1) * BLK] for p in range(slots)]
+            for p in (0, slots - 1):
+                tiles[p] = jnp.where(col <= row, tiles[p], NEG)
+            max_lo, max_hi = tiles[0], tiles[slots - 1]
+            for p in range(1, slots - 1):
                 if p < half:
-                    max_lo = jnp.maximum(max_lo, tiles[p] + (1.0 - in_lo[p]) * NEG)
-                    max_hi = jnp.maximum(max_hi, tiles[p] + in_lo[p] * NEG)
-                elif p > half:
-                    max_hi = jnp.maximum(max_hi, tiles[p])
+                    max_lo = jnp.maximum(max_lo, tiles[p] + bias_lo[p])
+                    max_hi = jnp.maximum(max_hi, tiles[p] + bias_hi[p])
+                else:
+                    max_hi = jnp.maximum(max_hi, tiles[p] + biases[p])
             max_lo = jnp.max(max_lo, axis=1, keepdims=True)
             max_hi = jnp.max(max_hi, axis=1, keepdims=True)
-
-            def pick(p, of_lo, of_hi):
-                if p == 0:
-                    return of_lo
-                if p >= half:
-                    return of_hi
-                return of_lo * in_lo[p] + of_hi * (1.0 - in_lo[p])
-
             sum_lo = sum_hi = None
             for p in range(slots):
-                tiles[p] = jnp.exp2((tiles[p] - pick(p, max_lo, max_hi)) * (SCALE * LOG2E))
+                top = pick(p, max_lo, max_hi)
+                if biases[p] is not None:
+                    top = top - biases[p]
+                tile = jnp.exp2((tiles[p] - top) * (SCALE * LOG2E))
+                s_buf[c % 2, inner, p * BLK : (p + 1) * BLK] = tile
+                prob[rows_at, p * BLK : (p + 1) * BLK] = tile.astype(jnp.bfloat16)
                 if p == 0:
-                    sum_lo = tiles[p]
+                    sum_lo = tile
                 elif p < half:
-                    sum_lo = sum_lo + tiles[p] * in_lo[p]
-                    part = tiles[p] * (1.0 - in_lo[p])
+                    sum_lo = sum_lo + jnp.where(is_lo[p], tile, 0.0)
+                    part = jnp.where(is_lo[p], 0.0, tile)
                     sum_hi = part if sum_hi is None else sum_hi + part
                 else:
-                    sum_hi = tiles[p] if sum_hi is None else sum_hi + tiles[p]
+                    sum_hi = tile if sum_hi is None else sum_hi + tile
             inv_lo = 1.0 / jnp.sum(sum_lo, axis=1, keepdims=True)
             inv_hi = 1.0 / jnp.sum(sum_hi, axis=1, keepdims=True)
-            for p in range(slots):
-                tiles[p] = tiles[p] * pick(p, inv_lo, inv_hi)
-                prob[at, p * BLK : (p + 1) * BLK] = tiles[p].astype(jnp.bfloat16)
+            for src, dst in ((qq, q_scaled), (gg, g_scaled)):
+                for cols, inv in ((slice(0, HEAD_SIZE), inv_lo), (slice(HEAD_SIZE, None), inv_hi)):
+                    dst[inner, cols] = (src[rows_at, cols].astype(jnp.float32) * inv).astype(
+                        jnp.bfloat16
+                    )
+            return inv_lo, inv_hi
+
+        def finish(c):
+            at = slice(c * ROWS_CHUNK, (c + 1) * ROWS_CHUNK)
+            inverses = [softmax(c, r) for r in range(0, ROWS_CHUNK, SUB)]
             wide = jnp.dot(prob[at, :], value_slots[...], preferred_element_type=jnp.float32)
-            att_now[0, at, :] = wide[:, :HEAD_SIZE].astype(jnp.bfloat16)
-            att_now[1, at, :] = wide[:, HEAD_SIZE:].astype(jnp.bfloat16)
-            dots = wide * gg[at, :].astype(jnp.float32)
-            dot_lo = jnp.sum(dots[:, :HEAD_SIZE], axis=1, keepdims=True)
-            dot_hi = jnp.sum(dots[:, HEAD_SIZE:], axis=1, keepdims=True)
-            dprob = lax.dot_general(
-                gg[at, :], value_slots[...], nt, preferred_element_type=jnp.float32
-            )
-            for p in range(slots):
-                cols = slice(p * BLK, (p + 1) * BLK)
-                dscore[at, cols] = (tiles[p] * (dprob[:, cols] - pick(p, dot_lo, dot_hi))).astype(
+            for src, dst in ((q_scaled, qq_t), (g_scaled, gg_t)):
+                dst[:, at] = src[...].T
+            for n, (inv_lo, inv_hi) in enumerate(inverses):
+                inner = slice(n * SUB, (n + 1) * SUB)
+                rows_at = slice(c * ROWS_CHUNK + n * SUB, c * ROWS_CHUNK + (n + 1) * SUB)
+                of_lo = wide[inner, :HEAD_SIZE] * inv_lo
+                of_hi = wide[inner, HEAD_SIZE:] * inv_hi
+                att_now[0, rows_at, :] = of_lo.astype(jnp.bfloat16)
+                att_now[1, rows_at, :] = of_hi.astype(jnp.bfloat16)
+                grad = gg[rows_at, :].astype(jnp.float32)
+                dot_lo = jnp.sum(of_lo * grad[:, :HEAD_SIZE], axis=1, keepdims=True)
+                dot_hi = jnp.sum(of_hi * grad[:, HEAD_SIZE:], axis=1, keepdims=True)
+                for p in range(slots):
+                    cols = slice(p * BLK, (p + 1) * BLK)
+                    dscore[rows_at, cols] = (
+                        s_buf[c % 2, inner, cols]
+                        * (d_buf[c % 2, inner, cols] - pick(p, dot_lo, dot_hi))
+                    ).astype(jnp.bfloat16)
+            dq = jnp.dot(dscore[at, :], key_slots[...], preferred_element_type=jnp.float32)
+            for n, (inv_lo, inv_hi) in enumerate(inverses):
+                inner = slice(n * SUB, (n + 1) * SUB)
+                rows_at = slice(c * ROWS_CHUNK + n * SUB, c * ROWS_CHUNK + (n + 1) * SUB)
+                dq_now[0, rows_at, :] = (dq[inner, :HEAD_SIZE] * (inv_lo * SCALE)).astype(
                     jnp.bfloat16
                 )
-            dq = SCALE * jnp.dot(dscore[at, :], key_slots[...], preferred_element_type=jnp.float32)
-            dq_now[0, at, :] = dq[:, :HEAD_SIZE].astype(jnp.bfloat16)
-            dq_now[1, at, :] = dq[:, HEAD_SIZE:].astype(jnp.bfloat16)
-            return carry
-
-        lax.fori_loop(0, rows // ROWS_CHUNK, one_chunk, 0)
+                dq_now[1, rows_at, :] = (dq[inner, HEAD_SIZE:] * (inv_hi * SCALE)).astype(
+                    jnp.bfloat16
+                )
+
+        matmuls(0)
+        for c in range(rows // ROWS_CHUNK):
+            if c + 1 < rows // ROWS_CHUNK:
+                matmuls(c + 1)
+            finish(c)
 
         @pl.when(h < heads - 1)
         def _():
@@ -366,7 +404,7 @@
 
         @pl.when(h > 0)
         def _():
-            second_stage(h - 1)
+            second_stage(h - 1, 0)
 
         for b in range(2):
             from_now = jnp.where(at_lo == b, 0, 1)
@@ -377,19 +415,6 @@
             out_copy(h, b, 0).start()
             out_copy(h, b, 1).start()
 
-        for i, (left, right) in enumerate(((qq_t, dscore), (gg_t, prob))):
-            grads = jnp.dot(left[...], right[...], preferred_element_type=jnp.float32)
-            for p in range(slots):
-                cols = slice(p * BLK, (p + 1) * BLK)
-                if p == 0:
-                    d_slots[i, p] = grads[:HEAD_SIZE, cols]
-                elif p >= half:
-                    d_slots[i, p] = grads[HEAD_SIZE:, cols]
-                else:
-                    d_slots[i, p] = grads[:HEAD_SIZE, cols] * in_lo[p] + grads[
-                        HEAD_SIZE:, cols
-                    ] * (1.0 - in_lo[p])
-
         def partial(i, target, b):
             seq = bt_ref[target, b]
             slot_lo = jnp.maximum(lo - seq, 0)
@@ -399,29 +424,33 @@
             of_hi = jnp.where(seq <= hi, jnp.float32(scale), jnp.float32(0))
             return (d_slots[i, slot_lo] * of_lo + d_slots[i, slot_hi] * of_hi).T
 
-        for i in range(2):
+        for i, left, right in ((1, gg_t, prob), (0, qq_t, dscore)):
+            grads = jnp.dot(left[...], right[...], preferred_element_type=jnp.float32)
+            for p in range(slots):
+                cols = slice(p * BLK, (p + 1) * BLK)
+                d_slots[i, p] = pick(p, grads[:HEAD_SIZE, cols], grads[HEAD_SIZE:, cols])
             for b in range(2):
                 at = slice(b * BLK, (b + 1) * BLK)
-                mate_send[h, 0, i, at] = partial(i, mate, b).astype(jnp.bfloat16)
-                mate_send[h, 1, i, at] = partial(i, cross, b).astype(jnp.bfloat16)
-        mate_copy(h).start()
-        for i in range(2):
+                mate_send[h, i, 0, at] = partial(i, mate, b).astype(jnp.bfloat16)
+                mate_send[h, i, 1, at] = partial(i, cross, b).astype(jnp.bfloat16)
+            mate_copy(h, i).start()
             for b in range(2):
                 at = slice(b * BLK, (b + 1) * BLK)
                 y_part[h, i, at] = partial(i, peer, b)
                 own_part[h, i, at] = partial(i, me, b)
+        second_stage(h, 1)
         return carry
 
     lax.fori_loop(0, heads, one_head, 0)
-    second_stage(heads - 1)
+    second_stage(heads - 1, 0)
 
     dkv_copies = []
-    for h in range(heads):
-        peer_copy(h).wait_recv()
-        for i, dst in enumerate((dk_hbm, dv_hbm)):
+    for i, dst in ((1, dv_hbm), (0, dk_hbm)):
+        for h in range(heads):
+            peer_copy(h, i).wait_recv()
             total = (
                 own_part[h, i]
-                + mate_recv[h, 0, i].astype(jnp.float32)
+                + mate_recv[h, i, 0].astype(jnp.float32)
                 + y_recv[h, i].astype(jnp.float32)
             )
             dkv_buf[h, i] = total.astype(jnp.bfloat16)
@@ -435,8 +464,9 @@
         gather_copy(h, me, peer, 0).wait_send()
         gather_copy(h, me, mate, 1).wait_send()
         gather_copy(h, peer, mate, 2).wait_send()
-        mate_copy(h).wait_send()
-        peer_copy(h).wait_send()
+        for i in range(2):
+            mate_copy(h, i).wait_send()
+            peer_copy(h, i).wait_send()
         for b in range(2):
             out_copy(h, b, 0).wait()
             out_copy(h, b, 1).wait()
@@ -467,8 +497,14 @@
         vmem((rows, pair), bf16),
         vmem((pair, rows), bf16),
         vmem((pair, rows), bf16),
+        vmem((ROWS_CHUNK, pair), bf16),
+        vmem((ROWS_CHUNK, pair), bf16),
         vmem((slots * BLK, pair), bf16),
         vmem((slots * BLK, pair), bf16),
+        vmem((pair, slots * BLK), bf16),
+        vmem((pair, slots * BLK), bf16),
+        vmem((2, ROWS_CHUNK, slots * BLK), f32),
+        vmem((2, ROWS_CHUNK, slots * BLK), f32),
         vmem((rows, slots * BLK), bf16),
         vmem((rows, slots * BLK), bf16),
         vmem((2, rows, HEAD_SIZE), bf16),
@@ -487,11 +523,11 @@
         dma((heads, 2)),
         dma((heads, 3)),
         dma((heads, 3)),
-        dma((heads, 2)),
-        dma((heads, 2)),
+        dma((heads, 2, 2)),
+        dma((heads, 2, 2)),
     ]
     smem = pl.BlockSpec(memory_space=pltpu.SMEM)
-    hbm = pl.BlockSpec(memory_space=pl.ANY)
+    hbm = pl.BlockSpec(memory_space=pltpu.HBM)
     return pl.pallas_call(
         functools.partial(fused_kernel, heads, groups, blocks),
         out_shape=(
@@ -504,7 +540,7 @@
         out_specs=(hbm, hbm, hbm, hbm),
         scratch_shapes=scratch,
         compiler_params=pltpu.CompilerParams(
-            collective_id=0, has_side_effects=True, vmem_limit_bytes=52 * 1024 * 1024
+            collective_id=0, has_side_effects=True, vmem_limit_bytes=56 * 1024 * 1024
         ),
         cost_estimate=pl.CostEstimate(
             flops=12 * heads * rows * pair * slots * BLK,

time: 67.6 us -> 54.7 us (0.81)
  Pallas kernels: 57.4 us -> 46.5 us
  local copies, waits for them, and re-layouts: 9.36 us -> 7.35 us
    pallas_call x1, Pallas kernels: 57.4 us -> 46.5 us  [per_device_fused(): pl.pallas_call(functools.partial(fused_kernel, heads, groups, blocks), ou...]
    unnamed x13 -> x11, local copies, waits for them, and re-layouts: 9.36 us -> 7.35 us
where the time goes in v2:
time: 54.7 us; the launch traced here: 54.5 us
  Pallas kernels  46.5 us (85%)
  local copies, waits for them, and re-layouts  7.35 us (13%)
  between operations  0.65 us (1%)
    pallas_call x1, Pallas kernels, per_device_fused(): pl.pallas_call(functools.partial(fused_kernel, heads, groups, blocks), ou...  46.5 us
    unnamed x11, local copies, waits for them, and re-layouts  7.35 us

profile of v2, /device:TPU:0, one launch (start us, length us, event | category | flops | bytes accessed | tf_op | source)
XLA Modules:
  0.0 54.5 jit_solution(16911700934156180927)
XLA Ops:
  0.6 1.3 %copy.10.bt_ref = s32[4,2]{1,0:T(4,128)} copy(s32[4,2]{0,1:T(2,128)} %param.10) | data formatting | bytes 64 | tf_op args[4]
  2.0 46.5 %shard_map.93 = (bf16[256,4096]{1,0:T(8,128)(2,1)}, bf16[256,4096]{1,0:T(8,128)(2,1)}, bf16[256,512]{1,0:T(8,128)(2,1)}, bf16[256,512]{1,0:T(8,128)(2,1)}) custom-call(s32[4,2]{1,0:T(4,128)} %copy.10.bt_ref, s32[8,10]{1,0:T(8,128)} %pat_ref.1, bf16[256,4096]{1,0:T(8,128)(2,1)} %q_hbm.1, bf16[256,512]{1,0:T(8,128)(2,1)} %k_hbm.1, bf16[256,512]{1,0:T(8,128)(2,1)} %v_hbm.1, ...), custom_call_target="tpu_custom_call" | custom-call | flops 14495514624 | bytes 9437184 | tf_op jit(solution)/shard_map/pallas_call | solution.py:531
  48.5 0.0 copy-start
  48.5 3.3 %copy.15 = bf16[256,4096]{1,0:T(8,128)(2,1)} copy(bf16[256,4096]{1,0:T(8,128)(2,1)} %get-tuple-element.8) | data formatting | bytes 4194304
  51.8 0.0 copy-done
  51.8 0.0 copy-start.2
  51.8 0.0 copy-start.1
  51.8 1.3 %copy.16 = bf16[256,4096]{1,0:T(8,128)(2,1)} copy(bf16[256,4096]{1,0:T(8,128)(2,1)S(1)} %copy-done) | data formatting | bytes 4194304
  53.1 0.0 copy-done.2
  53.1 0.7 %copy.17 = bf16[256,512]{1,0:T(8,128)(2,1)} copy(bf16[256,512]{1,0:T(8,128)(2,1)S(1)} %copy-done.2) | data formatting | bytes 524288
  53.8 0.0 copy-done.1
  53.8 0.7 %copy.18 = bf16[256,512]{1,0:T(8,128)(2,1)} copy(bf16[256,512]{1,0:T(8,128)(2,1)S(1)} %copy-done.1) | data formatting | bytes 524288
Async XLA Ops:
  48.5 3.3 %copy-start = (bf16[256,4096]{1,0:T(8,128)(2,1)S(1)}, bf16[256,4096]{1,0:T(8,128)(2,1)}, u32[]{:S(2)}) copy-start(bf16[256,4096]{1,0:T(8,128)(2,1)} %get-tuple-element.9) | copy-start | bytes 6291460
  51.8 1.3 %copy-start.2 = (bf16[256,512]{1,0:T(8,128)(2,1)S(1)}, bf16[256,512]{1,0:T(8,128)(2,1)}, u32[]{:S(2)}) copy-start(bf16[256,512]{1,0:T(8,128)(2,1)} %get-tuple-element.10) | copy-start | bytes 786436
  51.8 2.0 %copy-start.1 = (bf16[256,512]{1,0:T(8,128)(2,1)S(1)}, bf16[256,512]{1,0:T(8,128)(2,1)}, u32[]{:S(2)}) copy-start(bf16[256,512]{1,0:T(8,128)(2,1)} %get-tuple-element.11) | copy-start | bytes 786436

commit v3 on v2

--- a/solution.py
+++ b/solution.py
@@ -124,11 +124,11 @@
 def fused_kernel(
     heads, groups, blocks,
     bt_ref, pat_ref, q_hbm, k_hbm, v_hbm, g_hbm,
-    att_hbm, dq_hbm, dk_hbm, dv_hbm,
-    kv_all, kv_now, q_buf, g_buf, att_buf, dq_buf,
-    qq, gg, qq_t, gg_t, q_scaled, g_scaled, key_slots, value_slots, key_t, value_t, s_buf, d_buf, prob, dscore, att_now, dq_now,
-    d_slots, own_part, y_part, mate_send, mate_recv, y_send, y_recv, dkv_buf,
-    load_sem, kv_sem, out_sem, dkv_sem, gather_send, gather_recv, red_send, red_recv,
+    att_out, dq_out, dk_out, dv_out,
+    kv_all, kv_now, q_buf, g_buf,
+    qq, gg, qq_t, gg_t, q_scaled, g_scaled, key_slots, value_slots, key_t, value_t, s_buf, d_buf, dv_early, dk_early, prob, dscore, att_now, dq_now,
+    d_slots, own_part, y_part, mate_send, mate_recv, y_send, y_recv,
+    load_sem, kv_sem, gather_send, gather_recv, red_send, red_recv,
 ):
     slots = blocks + 1
     half = blocks // 2
@@ -162,18 +162,18 @@
         pl.semaphore_signal(barrier, inc=1, device_id={"ctx": other}, device_id_type=MESH)
     pl.semaphore_wait(barrier, 2)
 
-    def gather_copy(h, source, target, kind):
+    def gather_copy(h, i, source, target, kind):
         return pltpu.make_async_remote_copy(
-            src_ref=kv_all.at[h, :, source],
-            dst_ref=kv_all.at[h, :, source],
-            send_sem=gather_send.at[h, kind],
-            recv_sem=gather_recv.at[h, kind],
+            src_ref=kv_all.at[h, i, source],
+            dst_ref=kv_all.at[h, i, source],
+            send_sem=gather_send.at[h, i, kind],
+            recv_sem=gather_recv.at[h, i, kind],
             device_id={"ctx": target},
             device_id_type=MESH,
         )
 
-    def gather_arrival(h, source, kind):
-        return gather_copy(h, source, mate, kind)
+    def gather_arrival(h, i, source, kind):
+        return gather_copy(h, i, source, mate, kind)
 
     def mate_copy(h, i):
         return pltpu.make_async_remote_copy(
@@ -195,25 +195,17 @@
             device_id_type=MESH,
         )
 
-    def out_copy(h, b, i):
-        buf, dst = ((att_buf, att_hbm), (dq_buf, dq_hbm))[i]
-        return pltpu.make_async_copy(
-            buf.at[h, b],
-            dst.at[b * BLK : (b + 1) * BLK, pl.ds(pl.multiple_of(h * width, width), width)],
-            out_sem.at[h, b, i],
-        )
-
     for h in range(heads):
-        kv_loads[2 * h].wait()
-        kv_loads[2 * h + 1].wait()
-        gather_copy(h, me, peer, 0).start()
-        gather_copy(h, me, mate, 1).start()
-
-    seq0, seq1 = bt_ref[me, 0], bt_ref[me, 1]
+        for i in range(2):
+            kv_loads[2 * h + i].wait()
+            gather_copy(h, i, me, peer, 0).start()
+            gather_copy(h, i, me, mate, 1).start()
+
+    seq0, seq1 = bt_ref[0, me], bt_ref[1, me]
     lo, hi = jnp.minimum(seq0, seq1), jnp.maximum(seq0, seq1)
     at_lo = jnp.where(seq0 > seq1, 1, 0)
     at_hi = 1 - at_lo
-    table = [bt_ref[g // 2, g % 2] for g in range(blocks)]
+    table = [bt_ref[g % 2, g // 2] for g in range(blocks)]
     homes, biases, is_lo = [], [], []
     for p in range(slots):
         if p == 0:
@@ -254,16 +246,17 @@
     for copy in loads:
         copy.wait()
 
-    def forward(h):
-        gather_arrival(h, peer, 0).wait_recv()
-        gather_copy(h, peer, mate, 2).start()
+    def forward(h, i):
+        gather_arrival(h, i, peer, 0).wait_recv()
+        gather_copy(h, i, peer, mate, 2).start()
 
     def second_stage(h, i):
         mate_copy(h, i).wait_recv()
         y_send[h, i] = (y_part[h, i] + mate_recv[h, i, 1].astype(jnp.float32)).astype(jnp.bfloat16)
         peer_copy(h, i).start()
 
-    forward(0)
+    forward(0, 0)
+    forward(0, 1)
 
     def one_head(h, carry):
         first = pl.multiple_of(h * width, width)
@@ -274,8 +267,9 @@
                     tile = src[at, :, cols]
                     dst[g * BLK : (g + 1) * BLK, part * HEAD_SIZE : (part + 1) * HEAD_SIZE] = tile
 
-        gather_arrival(h, mate, 1).wait_recv()
-        gather_arrival(h, cross, 2).wait_recv()
+        for i in range(2):
+            gather_arrival(h, i, mate, 1).wait_recv()
+            gather_arrival(h, i, cross, 2).wait_recv()
         for i in range(2):
             for c in range(blocks // 2):
                 for b in range(2):
@@ -392,15 +386,26 @@
                     jnp.bfloat16
                 )
 
+        chunks = rows // ROWS_CHUNK
+        early = slice(0, rows // 2)
         matmuls(0)
-        for c in range(rows // ROWS_CHUNK):
-            if c + 1 < rows // ROWS_CHUNK:
+        for c in range(chunks):
+            if c + 1 < chunks:
                 matmuls(c + 1)
+            if c == chunks // 2:
+                dv_early[...] = jnp.dot(
+                    gg_t[:, early], prob[early, :], preferred_element_type=jnp.float32
+                )
+            if c == chunks - 1:
+                dk_early[...] = jnp.dot(
+                    qq_t[:, early], dscore[early, :], preferred_element_type=jnp.float32
+                )
             finish(c)
 
         @pl.when(h < heads - 1)
         def _():
-            forward(h + 1)
+            forward(h + 1, 0)
+            forward(h + 1, 1)
 
         @pl.when(h > 0)
         def _():
@@ -408,15 +413,14 @@
 
         for b in range(2):
             from_now = jnp.where(at_lo == b, 0, 1)
+            at = slice(b * BLK, (b + 1) * BLK)
             for g in range(groups):
-                cols = slice(g * HEAD_SIZE, (g + 1) * HEAD_SIZE)
-                att_buf[h, b, :, cols] = att_now[from_now, g * BLK : (g + 1) * BLK, :]
-                dq_buf[h, b, :, cols] = dq_now[from_now, g * BLK : (g + 1) * BLK, :]
-            out_copy(h, b, 0).start()
-            out_copy(h, b, 1).start()
+                cols = pl.ds(pl.multiple_of(first + g * HEAD_SIZE, HEAD_SIZE), HEAD_SIZE)
+                att_out[at, cols] = att_now[from_now, g * BLK : (g + 1) * BLK, :]
+                dq_out[at, cols] = dq_now[from_now, g * BLK : (g + 1) * BLK, :]
 
         def partial(i, target, b):
-            seq = bt_ref[target, b]
+            seq = bt_ref[b, target]
             slot_lo = jnp.maximum(lo - seq, 0)
             slot_hi = jnp.minimum(lo + 1 + seq, slots - 1)
             scale = SCALE if i == 0 else 1.0
@@ -424,8 +428,14 @@
             of_hi = jnp.where(seq <= hi, jnp.float32(scale), jnp.float32(0))
             return (d_slots[i, slot_lo] * of_lo + d_slots[i, slot_hi] * of_hi).T
 
-        for i, left, right in ((1, gg_t, prob), (0, qq_t, dscore)):
-            grads = jnp.dot(left[...], right[...], preferred_element_type=jnp.float32)
+        late = slice(rows // 2, rows)
+        for i, left, right, first_half in (
+            (1, gg_t, prob, dv_early),
+            (0, qq_t, dscore, dk_early),
+        ):
+            grads = first_half[...] + jnp.dot(
+                left[:, late], right[late, :], preferred_element_type=jnp.float32
+            )
             for p in range(slots):
                 cols = slice(p * BLK, (p + 1) * BLK)
                 d_slots[i, p] = pick(p, grads[:HEAD_SIZE, cols], grads[HEAD_SIZE:, cols])
@@ -444,8 +454,7 @@
     lax.fori_loop(0, heads, one_head, 0)
     second_stage(heads - 1, 0)
 
-    dkv_copies = []
-    for i, dst in ((1, dv_hbm), (0, dk_hbm)):
+    for i, dst in ((1, dv_out), (0, dk_out)):
         for h in range(heads):
             peer_copy(h, i).wait_recv()
             total = (
@@ -453,24 +462,24 @@
                 + mate_recv[h, i, 0].astype(jnp.float32)
                 + y_recv[h, i].astype(jnp.float32)
             )
-            dkv_buf[h, i] = total.astype(jnp.bfloat16)
-            copy = pltpu.make_async_copy(
-                dkv_buf.at[h, i], dst.at[:, h * HEAD_SIZE : (h + 1) * HEAD_SIZE], dkv_sem.at[h, i]
-            )
-            copy.start()
-            dkv_copies.append(copy)
+            dst[:, h * HEAD_SIZE : (h + 1) * HEAD_SIZE] = total.astype(jnp.bfloat16)
 
     for h in range(heads):
-        gather_copy(h, me, peer, 0).wait_send()
-        gather_copy(h, me, mate, 1).wait_send()
-        gather_copy(h, peer, mate, 2).wait_send()
         for i in range(2):
+            gather_copy(h, i, me, peer, 0).wait_send()
+            gather_copy(h, i, me, mate, 1).wait_send()
+            gather_copy(h, i, peer, mate, 2).wait_send()
             mate_copy(h, i).wait_send()
             peer_copy(h, i).wait_send()
-        for b in range(2):
-            out_copy(h, b, 0).wait()
-            out_copy(h, b, 1).wait()
-    for copy in dkv_copies:
+
+
+def write_kernel(*refs):
+    copies = [
+        pltpu.make_async_copy(refs[i], refs[4 + i], refs[8].at[i]) for i in range(4)
+    ]
+    for copy in copies:
+        copy.start()
+    for copy in copies:
         copy.wait()
 
 
@@ -491,8 +500,6 @@
         vmem((2, blocks, BLK, HEAD_SIZE), bf16),
         vmem((2, BLK, heads * width), bf16),
         vmem((2, BLK, heads * width), bf16),
-        vmem((heads, 2, BLK, width), bf16),
-        vmem((heads, 2, BLK, width), bf16),
         vmem((rows, pair), bf16),
         vmem((rows, pair), bf16),
         vmem((pair, rows), bf16),
@@ -505,6 +512,8 @@
         vmem((pair, slots * BLK), bf16),
         vmem((2, ROWS_CHUNK, slots * BLK), f32),
         vmem((2, ROWS_CHUNK, slots * BLK), f32),
+        vmem((pair, slots * BLK), f32),
+        vmem((pair, slots * BLK), f32),
         vmem((rows, slots * BLK), bf16),
         vmem((rows, slots * BLK), bf16),
         vmem((2, rows, HEAD_SIZE), bf16),
@@ -516,38 +525,39 @@
         vmem((heads, 2, 2, held, HEAD_SIZE), bf16),
         vmem((heads, 2, held, HEAD_SIZE), bf16),
         vmem((heads, 2, held, HEAD_SIZE), bf16),
-        vmem((heads, 2, held, HEAD_SIZE), bf16),
         dma((2, 2)),
         dma((heads, 2)),
-        dma((heads, 2, 2)),
-        dma((heads, 2)),
-        dma((heads, 3)),
-        dma((heads, 3)),
+        dma((heads, 2, 3)),
+        dma((heads, 2, 3)),
         dma((heads, 2, 2)),
         dma((heads, 2, 2)),
     ]
     smem = pl.BlockSpec(memory_space=pltpu.SMEM)
     hbm = pl.BlockSpec(memory_space=pltpu.HBM)
-    return pl.pallas_call(
+    on_chip = pl.BlockSpec(memory_space=pltpu.VMEM)
+    out_shapes = (query_rows.shape, query_rows.shape, key_rows.shape, key_rows.shape)
+    results = pl.pallas_call(
         functools.partial(fused_kernel, heads, groups, blocks),
-        out_shape=(
-            jax.ShapeDtypeStruct(query_rows.shape, bf16),
-            jax.ShapeDtypeStruct(query_rows.shape, bf16),
-            jax.ShapeDtypeStruct(key_rows.shape, bf16),
-            jax.ShapeDtypeStruct(key_rows.shape, bf16),
-        ),
+        out_shape=tuple(vmem(shape, bf16) for shape in out_shapes),
         in_specs=[smem, smem, hbm, hbm, hbm, hbm],
-        out_specs=(hbm, hbm, hbm, hbm),
+        out_specs=(on_chip,) * 4,
         scratch_shapes=scratch,
         compiler_params=pltpu.CompilerParams(
-            collective_id=0, has_side_effects=True, vmem_limit_bytes=56 * 1024 * 1024
+            collective_id=0, has_side_effects=True, vmem_limit_bytes=48 * 1024 * 1024
         ),
         cost_estimate=pl.CostEstimate(
             flops=12 * heads * rows * pair * slots * BLK,
             bytes_accessed=8 * query_rows.size + 8 * key_rows.size,
             transcendentals=heads * rows * slots * BLK,
         ),
-    )(block_table, pattern, query_rows, key_rows, stored_value_rows, out_grad)
+    )(block_table.T, pattern, query_rows, key_rows, stored_value_rows, out_grad)
+    return pl.pallas_call(
+        write_kernel,
+        out_shape=tuple(jax.ShapeDtypeStruct(shape, bf16) for shape in out_shapes),
+        in_specs=[on_chip] * 4,
+        out_specs=(hbm,) * 4,
+        scratch_shapes=[dma((4,))],
+    )(*results)
 
 
 def solution(mesh):

time: 54.7 us -> 59.1 us (1.080)
  Pallas kernels: 46.5 us -> 50.9 us
    pallas_call x0 -> x1, Pallas kernels: none -> 4.48 us  [per_device_fused(): pl.pallas_call(write_kernel, out_shape=tuple((jax.ShapeDtypeStruct(shape,...]
    unnamed x11 -> x16, local copies, waits for them, and re-layouts: 7.35 us -> 7.32 us
where the time goes in v3:
time: 59.1 us; the launch traced here: 58.9 us
  Pallas kernels  50.9 us (86%)
  local copies, waits for them, and re-layouts  7.32 us (12%)
  between operations  0.66 us (1%)
    pallas_call x1, Pallas kernels, per_device_fused(): pl.pallas_call(functools.partial(fused_kernel, heads, groups, blocks), ou...  46.4 us
    unnamed x16, local copies, waits for them, and re-layouts  7.32 us
    pallas_call x1, Pallas kernels, per_device_fused(): pl.pallas_call(write_kernel, out_shape=tuple((jax.ShapeDtypeStruct(shape,...  4.48 us

profile of v3, /device:TPU:0, one launch (start us, length us, event | category | flops | bytes accessed | tf_op | source)
XLA Modules:
  0.0 58.9 jit_solution(13377285375518390077)
XLA Ops:
  0.6 0.0 copy-start.4
  0.6 0.9 %copy-done.4 = bf16[256,512]{1,0:T(8,128)(2,1)S(1)} copy-done((bf16[256,512]{1,0:T(8,128)(2,1)S(1)}, bf16[256,512]{1,0:T(8,128)(2,1)}, u32[]{:S(2)}) %copy-start.4) | copy-done | bytes 262168
  1.6 0.0 copy-start.5
  1.6 0.9 %copy-done.5 = bf16[256,512]{1,0:T(8,128)(2,1)S(1)} copy-done((bf16[256,512]{1,0:T(8,128)(2,1)S(1)}, bf16[256,512]{1,0:T(8,128)(2,1)}, u32[]{:S(2)}) %copy-start.5) | copy-done | bytes 262168
  2.5 0.0 copy-start.6
  2.5 0.7 %copy-done.6 = s32[8,10]{1,0:T(8,128)S(1)} copy-done((s32[8,10]{1,0:T(8,128)S(1)}, s32[8,10]{1,0:T(8,128)}, u32[]{:S(2)}) %copy-start.6) | copy-done | bytes 344
  3.2 0.0 copy-start.7
  3.2 0.7 %copy-done.7 = s32[4,2]{0,1:T(2,128)S(1)} copy-done((s32[4,2]{0,1:T(2,128)S(1)}, s32[4,2]{0,1:T(2,128)}, u32[]{:S(2)}) %copy-start.7) | copy-done | bytes 56
  3.9 46.4 %shard_map.93 = (bf16[256,4096]{1,0:T(8,128)(2,1)S(1)}, bf16[256,4096]{1,0:T(8,128)(2,1)S(1)}, bf16[256,512]{1,0:T(8,128)(2,1)S(1)}, bf16[256,512]{1,0:T(8,128)(2,1)S(1)}) custom-call(s32[2,4]{1,0:T(2,128)S(1)} %bitcast.1, s32[8,10]{1,0:T(8,128)S(1)} %copy-done.6, bf16[256,4096]{1,0:T(8,128)(2,1)} %q_hbm.1, bf16[256,512]{1,0:T(8,128)(2,1)S(1)} %copy-done.4, ...), custom_call_target="tpu_custom_call" | custom-call | flops 14495514624 | bytes 9437184 | tf_op jit(solution)/shard_map/pallas_call | solution.py:539
  50.3 0.0 copy-start
  50.3 1.3 %copy-done = bf16[256,4096]{1,0:T(8,128)(2,1)} copy-done((bf16[256,4096]{1,0:T(8,128)(2,1)}, bf16[256,4096]{1,0:T(8,128)(2,1)S(1)}, u32[]{:S(2)}) %copy-start) | copy-done | bytes 2097176
  51.6 0.0 copy-start.1
  51.6 1.3 %copy-done.1 = bf16[256,4096]{1,0:T(8,128)(2,1)} copy-done((bf16[256,4096]{1,0:T(8,128)(2,1)}, bf16[256,4096]{1,0:T(8,128)(2,1)S(1)}, u32[]{:S(2)}) %copy-start.1) | copy-done | bytes 2097176
  53.0 0.0 copy-start.2
  53.0 0.7 %copy-done.2 = bf16[256,512]{1,0:T(8,128)(2,1)} copy-done((bf16[256,512]{1,0:T(8,128)(2,1)}, bf16[256,512]{1,0:T(8,128)(2,1)S(1)}, u32[]{:S(2)}) %copy-start.2) | copy-done | bytes 262168
  53.7 0.0 copy-start.3
  53.7 0.7 %copy-done.3 = bf16[256,512]{1,0:T(8,128)(2,1)} copy-done((bf16[256,512]{1,0:T(8,128)(2,1)}, bf16[256,512]{1,0:T(8,128)(2,1)S(1)}, u32[]{:S(2)}) %copy-start.3) | copy-done | bytes 262168
  54.4 4.5 %shard_map.94 = (bf16[256,4096]{1,0:T(8,128)(2,1)}, bf16[256,4096]{1,0:T(8,128)(2,1)}, bf16[256,512]{1,0:T(8,128)(2,1)}, bf16[256,512]{1,0:T(8,128)(2,1)}) custom-call(bf16[256,4096]{1,0:T(8,128)(2,1)} %copy-done, bf16[256,4096]{1,0:T(8,128)(2,1)} %copy-done.1, bf16[256,512]{1,0:T(8,128)(2,1)} %copy-done.2, bf16[256,512]{1,0:T(8,128)(2,1)} %copy-done.3), custom_call_target="tpu_custom_call" | custom-call | tf_op jit(solution)/shard_map/pallas_call | solution.py:554
Async XLA Ops:
  0.6 1.0 %copy-start.4 = (bf16[256,512]{1,0:T(8,128)(2,1)S(1)}, bf16[256,512]{1,0:T(8,128)(2,1)}, u32[]{:S(2)}) copy-start(bf16[256,512]{1,0:T(8,128)(2,1)} %k_hbm.1) | copy-start | bytes 786436
  1.6 0.9 %copy-start.5 = (bf16[256,512]{1,0:T(8,128)(2,1)S(1)}, bf16[256,512]{1,0:T(8,128)(2,1)}, u32[]{:S(2)}) copy-start(bf16[256,512]{1,0:T(8,128)(2,1)} %v_hbm.1) | copy-start | bytes 786436
  2.5 0.7 %copy-start.6 = (s32[8,10]{1,0:T(8,128)S(1)}, s32[8,10]{1,0:T(8,128)}, u32[]{:S(2)}) copy-start(s32[8,10]{1,0:T(8,128)} %pat_ref.1) | copy-start | bytes 964
  3.2 0.7 %copy-start.7 = (s32[4,2]{0,1:T(2,128)S(1)}, s32[4,2]{0,1:T(2,128)}, u32[]{:S(2)}) copy-start(s32[4,2]{0,1:T(2,128)} %param.10) | copy-start | bytes 100
  50.3 1.3 %copy-start = (bf16[256,4096]{1,0:T(8,128)(2,1)}, bf16[256,4096]{1,0:T(8,128)(2,1)S(1)}, u32[]{:S(2)}) copy-start(bf16[256,4096]{1,0:T(8,128)(2,1)S(1)} %get-tuple-element.8.refs_0_) | copy-start | bytes 6291460
  51.6 1.3 %copy-start.1 = (bf16[256,4096]{1,0:T(8,128)(2,1)}, bf16[256,4096]{1,0:T(8,128)(2,1)S(1)}, u32[]{:S(2)}) copy-start(bf16[256,4096]{1,0:T(8,128)(2,1)S(1)} %get-tuple-element.9.refs_1_) | copy-start | bytes 6291460
  53.0 0.7 %copy-start.2 = (bf16[256,512]{1,0:T(8,128)(2,1)}, bf16[256,512]{1,0:T(8,128)(2,1)S(1)}, u32[]{:S(2)}) copy-start(bf16[256,512]{1,0:T(8,128)(2,1)S(1)} %get-tuple-element.10.refs_2_) | copy-start | bytes 786436
  53.7 0.7 %copy-start.3 = (bf16[256,512]{1,0:T(8,128)(2,1)}, bf16[256,512]{1,0:T(8,128)(2,1)S(1)}, u32[]{:S(2)}) copy-start(bf16[256,512]{1,0:T(8,128)(2,1)S(1)} %get-tuple-element.11.refs_3_) | copy-start | bytes 786436

commit v4 on v3

--- a/solution.py
+++ b/solution.py
@@ -10,7 +10,7 @@
 HEAD_SIZE = 128
 BLK = 128
 MESH = pl.DeviceIdType.MESH
-ROWS_CHUNK = 256
+ROWS_CHUNK = 512
 SUB = 32
 NEG = -1e30
 SCALE = HEAD_SIZE ** (-0.5)
@@ -124,11 +124,11 @@
 def fused_kernel(
     heads, groups, blocks,
     bt_ref, pat_ref, q_hbm, k_hbm, v_hbm, g_hbm,
-    att_out, dq_out, dk_out, dv_out,
-    kv_all, kv_now, q_buf, g_buf,
+    att_hbm, dq_hbm, dk_hbm, dv_hbm,
+    kv_all, kv_now, q_buf, g_buf, att_buf, dq_buf,
     qq, gg, qq_t, gg_t, q_scaled, g_scaled, key_slots, value_slots, key_t, value_t, s_buf, d_buf, dv_early, dk_early, prob, dscore, att_now, dq_now,
-    d_slots, own_part, y_part, mate_send, mate_recv, y_send, y_recv,
-    load_sem, kv_sem, gather_send, gather_recv, red_send, red_recv,
+    d_slots, own_part, y_part, mate_send, mate_recv, y_send, y_recv, dkv_buf,
+    load_sem, kv_sem, out_sem, dkv_sem, gather_send, gather_recv, red_send, red_recv,
 ):
     slots = blocks + 1
     half = blocks // 2
@@ -193,6 +193,14 @@
             recv_sem=red_recv.at[h, 1, i],
             device_id={"ctx": peer},
             device_id_type=MESH,
+        )
+
+    def out_copy(h, b, i):
+        buf, dst = ((att_buf, att_hbm), (dq_buf, dq_hbm))[i]
+        return pltpu.make_async_copy(
+            buf.at[h, b],
+            dst.at[b * BLK : (b + 1) * BLK, pl.ds(pl.multiple_of(h * width, width), width)],
+            out_sem.at[h, b, i],
         )
 
     for h in range(heads):
@@ -413,11 +421,12 @@
 
         for b in range(2):
             from_now = jnp.where(at_lo == b, 0, 1)
-            at = slice(b * BLK, (b + 1) * BLK)
             for g in range(groups):
-                cols = pl.ds(pl.multiple_of(first + g * HEAD_SIZE, HEAD_SIZE), HEAD_SIZE)
-                att_out[at, cols] = att_now[from_now, g * BLK : (g + 1) * BLK, :]
-                dq_out[at, cols] = dq_now[from_now, g * BLK : (g + 1) * BLK, :]
+                cols = slice(g * HEAD_SIZE, (g + 1) * HEAD_SIZE)
+                att_buf[h, b, :, cols] = att_now[from_now, g * BLK : (g + 1) * BLK, :]
+                dq_buf[h, b, :, cols] = dq_now[from_now, g * BLK : (g + 1) * BLK, :]
+            out_copy(h, b, 0).start()
+            out_copy(h, b, 1).start()
 
         def partial(i, target, b):
             seq = bt_ref[b, target]
@@ -426,7 +435,7 @@
             scale = SCALE if i == 0 else 1.0
             of_lo = jnp.where(seq <= lo, jnp.float32(scale), jnp.float32(0))
             of_hi = jnp.where(seq <= hi, jnp.float32(scale), jnp.float32(0))
-            return (d_slots[i, slot_lo] * of_lo + d_slots[i, slot_hi] * of_hi).T
+            return d_slots[i, slot_lo] * of_lo + d_slots[i, slot_hi] * of_hi
 
         late = slice(rows // 2, rows)
         for i, left, right, first_half in (
@@ -454,15 +463,23 @@
     lax.fori_loop(0, heads, one_head, 0)
     second_stage(heads - 1, 0)
 
-    for i, dst in ((1, dv_out), (0, dk_out)):
-        for h in range(heads):
+    dkv_copies = []
+    for h in range(heads):
+        for i, dst in ((1, dv_hbm), (0, dk_hbm)):
             peer_copy(h, i).wait_recv()
             total = (
                 own_part[h, i]
                 + mate_recv[h, i, 0].astype(jnp.float32)
                 + y_recv[h, i].astype(jnp.float32)
             )
-            dst[:, h * HEAD_SIZE : (h + 1) * HEAD_SIZE] = total.astype(jnp.bfloat16)
+            for b in range(2):
+                at = slice(b * BLK, (b + 1) * BLK)
+                dkv_buf[h, i, at] = total[at].T.astype(jnp.bfloat16)
+            copy = pltpu.make_async_copy(
+                dkv_buf.at[h, i], dst.at[:, h * HEAD_SIZE : (h + 1) * HEAD_SIZE], dkv_sem.at[h, i]
+            )
+            copy.start()
+            dkv_copies.append(copy)
 
     for h in range(heads):
         for i in range(2):
@@ -471,12 +488,21 @@
             gather_copy(h, i, peer, mate, 2).wait_send()
             mate_copy(h, i).wait_send()
             peer_copy(h, i).wait_send()
+        for b in range(2):
+            out_copy(h, b, 0).wait()
+            out_copy(h, b, 1).wait()
+    for copy in dkv_copies:
+        copy.wait()
 
 
 def write_kernel(*refs):
-    copies = [
-        pltpu.make_async_copy(refs[i], refs[4 + i], refs[8].at[i]) for i in range(4)
-    ]
+    copies = []
+    for i in range(4):
+        src, dst = refs[i], refs[4 + i]
+        part = src.shape[0] // 4
+        for n in range(4):
+            at = slice(n * part, (n + 1) * part)
+            copies.append(pltpu.make_async_copy(src.at[at], dst.at[at], refs[8].at[i, n]))
     for copy in copies:
         copy.start()
     for copy in copies:
@@ -500,6 +526,8 @@
         vmem((2, blocks, BLK, HEAD_SIZE), bf16),
         vmem((2, BLK, heads * width), bf16),
         vmem((2, BLK, heads * width), bf16),
+        vmem((heads, 2, BLK, width), bf16),
+        vmem((heads, 2, BLK, width), bf16),
         vmem((rows, pair), bf16),
         vmem((rows, pair), bf16),
         vmem((pair, rows), bf16),
@@ -525,7 +553,10 @@
         vmem((heads, 2, 2, held, HEAD_SIZE), bf16),
         vmem((heads, 2, held, HEAD_SIZE), bf16),
         vmem((heads, 2, held, HEAD_SIZE), bf16),
+        vmem((heads, 2, held, HEAD_SIZE), bf16),
         dma((2, 2)),
+        dma((heads, 2)),
+        dma((heads, 2, 2)),
         dma((heads, 2)),
         dma((heads, 2, 3)),
         dma((heads, 2, 3)),
@@ -534,16 +565,15 @@
     ]
     smem = pl.BlockSpec(memory_space=pltpu.SMEM)
     hbm = pl.BlockSpec(memory_space=pltpu.HBM)
-    on_chip = pl.BlockSpec(memory_space=pltpu.VMEM)
     out_shapes = (query_rows.shape, query_rows.shape, key_rows.shape, key_rows.shape)
     results = pl.pallas_call(
         functools.partial(fused_kernel, heads, groups, blocks),
-        out_shape=tuple(vmem(shape, bf16) for shape in out_shapes),
+        out_shape=tuple(jax.ShapeDtypeStruct(shape, bf16) for shape in out_shapes),
         in_specs=[smem, smem, hbm, hbm, hbm, hbm],
-        out_specs=(on_chip,) * 4,
+        out_specs=(hbm, hbm, hbm, hbm),
         scratch_shapes=scratch,
         compiler_params=pltpu.CompilerParams(
-            collective_id=0, has_side_effects=True, vmem_limit_bytes=48 * 1024 * 1024
+            collective_id=0, has_side_effects=True, vmem_limit_bytes=56 * 1024 * 1024
         ),
         cost_estimate=pl.CostEstimate(
             flops=12 * heads * rows * pair * slots * BLK,
@@ -554,9 +584,10 @@
     return pl.pallas_call(
         write_kernel,
         out_shape=tuple(jax.ShapeDtypeStruct(shape, bf16) for shape in out_shapes),
-        in_specs=[on_chip] * 4,
+        in_specs=[hbm] * 4,
         out_specs=(hbm,) * 4,
-        scratch_shapes=[dma((4,))],
+        scratch_shapes=[dma((4, 4))],
+        compiler_params=pltpu.CompilerParams(vmem_limit_bytes=56 * 1024 * 1024),
     )(*results)
 
 

time: 59.1 us -> 193 us (3.27)
  Pallas kernels: 50.9 us -> 192 us
  local copies, waits for them, and re-layouts: 7.32 us -> 0 us
    pallas_call x1, Pallas kernels: 4.48 us -> 144 us  [per_device_fused(): pl.pallas_call(write_kernel, out_shape=tuple((jax.ShapeDtypeStruct(shape,...]
    unnamed x16 -> x0, local copies, waits for them, and re-layouts: 7.32 us -> none
where the time goes in v4:
time: 193 us
  Pallas kernels  192 us (99%)
    pallas_call x1, Pallas kernels, per_device_fused(): pl.pallas_call(write_kernel, out_shape=tuple((jax.ShapeDtypeStruct(shape,...  144 us
    pallas_call x1, Pallas kernels, per_device_fused(): pl.pallas_call(functools.partial(fused_kernel, heads, groups, blocks), ou...  48.2 us

profile of v4, /device:TPU:0, one launch (start us, length us, event | category | flops | bytes accessed | tf_op | source)
XLA Modules:
  0.0 193.0 jit_solution(6302754854635887644)
XLA Ops:
  0.6 48.2 %shard_map.93 = (bf16[256,4096]{1,0:T(8,128)(2,1)}, bf16[256,4096]{1,0:T(8,128)(2,1)}, bf16[256,512]{1,0:T(8,128)(2,1)}, bf16[256,512]{1,0:T(8,128)(2,1)}) custom-call(s32[2,4]{1,0:T(2,128)} %bitcast.1, s32[8,10]{1,0:T(8,128)} %pat_ref.1, bf16[256,4096]{1,0:T(8,128)(2,1)} %q_hbm.1, bf16[256,512]{1,0:T(8,128)(2,1)} %k_hbm.1, bf16[256,512]{1,0:T(8,128)(2,1)} %v_hbm.1, ...), custom_call_target="tpu_custom_call" | custom-call | flops 14495514624 | bytes 9437184 | tf_op jit(solution)/shard_map/pallas_call | solution.py:569
  48.8 144.2 %shard_map.94 = (bf16[256,4096]{1,0:T(8,128)(2,1)}, bf16[256,4096]{1,0:T(8,128)(2,1)}, bf16[256,512]{1,0:T(8,128)(2,1)}, bf16[256,512]{1,0:T(8,128)(2,1)}) custom-call(bf16[256,4096]{1,0:T(8,128)(2,1)} %get-tuple-element.8.refs_0_, bf16[256,4096]{1,0:T(8,128)(2,1)} %get-tuple-element.9.refs_1_, bf16[256,512]{1,0:T(8,128)(2,1)} %get-tuple-element.10.refs_2_, ...), custom_call_target="tpu_custom_call" | custom-call | tf_op jit(solution)/shard_map/pallas_call | solution.py:584

commit v5 on v4

--- a/solution.py
+++ b/solution.py
@@ -10,7 +10,7 @@
 HEAD_SIZE = 128
 BLK = 128
 MESH = pl.DeviceIdType.MESH
-ROWS_CHUNK = 512
+ROWS_CHUNK = 256
 SUB = 32
 NEG = -1e30
 SCALE = HEAD_SIZE ** (-0.5)
@@ -309,8 +309,8 @@
 
         def matmuls(c):
             at = slice(c * ROWS_CHUNK, (c + 1) * ROWS_CHUNK)
-            s_buf[c % 2] = jnp.dot(qq[at, :], key_t[...], preferred_element_type=jnp.float32)
-            d_buf[c % 2] = jnp.dot(gg[at, :], value_t[...], preferred_element_type=jnp.float32)
+            s_buf[c % 3] = jnp.dot(qq[at, :], key_t[...], preferred_element_type=jnp.float32)
+            d_buf[c % 3] = jnp.dot(gg[at, :], value_t[...], preferred_element_type=jnp.float32)
 
         def pick(p, of_lo, of_hi):
             if p == 0:
@@ -324,7 +324,7 @@
             inner = slice(r, r + SUB)
             row = lax.broadcasted_iota(jnp.int32, (SUB, BLK), 0) + (c * ROWS_CHUNK + r) % BLK
             col = lax.broadcasted_iota(jnp.int32, (SUB, BLK), 1)
-            tiles = [s_buf[c % 2, inner, p * BLK : (p + 1) * BLK] for p in range(slots)]
+            tiles = [s_buf[c % 3, inner, p * BLK : (p + 1) * BLK] for p in range(slots)]
             for p in (0, slots - 1):
                 tiles[p] = jnp.where(col <= row, tiles[p], NEG)
             max_lo, max_hi = tiles[0], tiles[slots - 1]
@@ -342,7 +342,7 @@
                 if biases[p] is not None:
                     top = top - biases[p]
                 tile = jnp.exp2((tiles[p] - top) * (SCALE * LOG2E))
-                s_buf[c % 2, inner, p * BLK : (p + 1) * BLK] = tile
+                s_buf[c % 3, inner, p * BLK : (p + 1) * BLK] = tile
                 prob[rows_at, p * BLK : (p + 1) * BLK] = tile.astype(jnp.bfloat16)
                 if p == 0:
                     sum_lo = tile
@@ -356,17 +356,22 @@
             inv_hi = 1.0 / jnp.sum(sum_hi, axis=1, keepdims=True)
             for src, dst in ((qq, q_scaled), (gg, g_scaled)):
                 for cols, inv in ((slice(0, HEAD_SIZE), inv_lo), (slice(HEAD_SIZE, None), inv_hi)):
-                    dst[inner, cols] = (src[rows_at, cols].astype(jnp.float32) * inv).astype(
+                    dst[c % 2, inner, cols] = (src[rows_at, cols].astype(jnp.float32) * inv).astype(
                         jnp.bfloat16
                     )
             return inv_lo, inv_hi
 
-        def finish(c):
+        def all_softmax(c):
+            return [softmax(c, r) for r in range(0, ROWS_CHUNK, SUB)]
+
+        def attend(c):
             at = slice(c * ROWS_CHUNK, (c + 1) * ROWS_CHUNK)
-            inverses = [softmax(c, r) for r in range(0, ROWS_CHUNK, SUB)]
-            wide = jnp.dot(prob[at, :], value_slots[...], preferred_element_type=jnp.float32)
+            return jnp.dot(prob[at, :], value_slots[...], preferred_element_type=jnp.float32)
+
+        def score_grads(c, wide, inverses):
+            at = slice(c * ROWS_CHUNK, (c + 1) * ROWS_CHUNK)
             for src, dst in ((q_scaled, qq_t), (g_scaled, gg_t)):
-                dst[:, at] = src[...].T
+                dst[:, at] = src[c % 2].T
             for n, (inv_lo, inv_hi) in enumerate(inverses):
                 inner = slice(n * SUB, (n + 1) * SUB)
                 rows_at = slice(c * ROWS_CHUNK + n * SUB, c * ROWS_CHUNK + (n + 1) * SUB)
@@ -380,9 +385,12 @@
                 for p in range(slots):
                     cols = slice(p * BLK, (p + 1) * BLK)
                     dscore[rows_at, cols] = (
-                        s_buf[c % 2, inner, cols]
-                        * (d_buf[c % 2, inner, cols] - pick(p, dot_lo, dot_hi))
+                        s_buf[c % 3, inner, cols]
+                        * (d_buf[c % 3, inner, cols] - pick(p, dot_lo, dot_hi))
                     ).astype(jnp.bfloat16)
+
+        def query_grads(c, inverses):
+            at = slice(c * ROWS_CHUNK, (c + 1) * ROWS_CHUNK)
             dq = jnp.dot(dscore[at, :], key_slots[...], preferred_element_type=jnp.float32)
             for n, (inv_lo, inv_hi) in enumerate(inverses):
                 inner = slice(n * SUB, (n + 1) * SUB)
@@ -397,18 +405,24 @@
         chunks = rows // ROWS_CHUNK
         early = slice(0, rows // 2)
         matmuls(0)
+        matmuls(1)
+        inverses = all_softmax(0)
         for c in range(chunks):
-            if c + 1 < chunks:
-                matmuls(c + 1)
+            wide = attend(c)
             if c == chunks // 2:
                 dv_early[...] = jnp.dot(
                     gg_t[:, early], prob[early, :], preferred_element_type=jnp.float32
                 )
+            later = all_softmax(c + 1) if c + 1 < chunks else None
+            if c + 2 < chunks:
+                matmuls(c + 2)
             if c == chunks - 1:
                 dk_early[...] = jnp.dot(
                     qq_t[:, early], dscore[early, :], preferred_element_type=jnp.float32
                 )
-            finish(c)
+            score_grads(c, wide, inverses)
+            query_grads(c, inverses)
+            inverses = later
 
         @pl.when(h < heads - 1)
         def _():
@@ -496,16 +510,20 @@
 
 
 def write_kernel(*refs):
-    copies = []
+    reads, writes = [], []
     for i in range(4):
-        src, dst = refs[i], refs[4 + i]
+        src, dst, held = refs[i], refs[4 + i], refs[8 + i]
         part = src.shape[0] // 4
         for n in range(4):
             at = slice(n * part, (n + 1) * part)
-            copies.append(pltpu.make_async_copy(src.at[at], dst.at[at], refs[8].at[i, n]))
-    for copy in copies:
+            reads.append(pltpu.make_async_copy(src.at[at], held.at[at], refs[12].at[i, n]))
+            writes.append(pltpu.make_async_copy(held.at[at], dst.at[at], refs[13].at[i, n]))
+    for copy in reads:
         copy.start()
-    for copy in copies:
+    for read, write in zip(reads, writes):
+        read.wait()
+        write.start()
+    for copy in writes:
         copy.wait()
 
 
@@ -532,14 +550,14 @@
         vmem((rows, pair), bf16),
         vmem((pair, rows), bf16),
         vmem((pair, rows), bf16),
-        vmem((ROWS_CHUNK, pair), bf16),
-        vmem((ROWS_CHUNK, pair), bf16),
+        vmem((2, ROWS_CHUNK, pair), bf16),
+        vmem((2, ROWS_CHUNK, pair), bf16),
         vmem((slots * BLK, pair), bf16),
         vmem((slots * BLK, pair), bf16),
         vmem((pair, slots * BLK), bf16),
         vmem((pair, slots * BLK), bf16),
-        vmem((2, ROWS_CHUNK, slots * BLK), f32),
-        vmem((2, ROWS_CHUNK, slots * BLK), f32),
+        vmem((3, ROWS_CHUNK, slots * BLK), f32),
+        vmem((3, ROWS_CHUNK, slots * BLK), f32),
         vmem((pair, slots * BLK), f32),
         vmem((pair, slots * BLK), f32),
         vmem((rows, slots * BLK), bf16),
@@ -586,7 +604,7 @@
         out_shape=tuple(jax.ShapeDtypeStruct(shape, bf16) for shape in out_shapes),
         in_specs=[hbm] * 4,
         out_specs=(hbm,) * 4,
-        scratch_shapes=[dma((4, 4))],
+        scratch_shapes=[vmem(shape, bf16) for shape in out_shapes] + [dma((4, 4)), dma((4, 4))],
         compiler_params=pltpu.CompilerParams(vmem_limit_bytes=56 * 1024 * 1024),
     )(*results)
 

time: 193 us -> 50.8 us (0.26)
  Pallas kernels: 192 us -> 49.9 us
    pallas_call x1, Pallas kernels: 144 us -> 4.05 us  [per_device_fused(): pl.pallas_call(write_kernel, out_shape=tuple((jax.ShapeDtypeStruct(shape,...]
    pallas_call x1, Pallas kernels: 48.2 us -> 45.9 us  [per_device_fused(): pl.pallas_call(functools.partial(fused_kernel, heads, groups, blocks), ou...]
where the time goes in v5:
time: 50.8 us; the launch traced here: 50.6 us
  Pallas kernels  49.9 us (98%)
  between operations  0.64 us (1%)
    pallas_call x1, Pallas kernels, per_device_fused(): pl.pallas_call(functools.partial(fused_kernel, heads, groups, blocks), ou...  45.9 us
    pallas_call x1, Pallas kernels, per_device_fused(): pl.pallas_call(write_kernel, out_shape=tuple((jax.ShapeDtypeStruct(shape,...  4.05 us

profile of v5, /device:TPU:0, one launch (start us, length us, event | category | flops | bytes accessed | tf_op | source)
XLA Modules:
  0.0 50.6 jit_solution(11397247537362356198)
XLA Ops:
  0.6 45.9 %shard_map.93 = (bf16[256,4096]{1,0:T(8,128)(2,1)}, bf16[256,4096]{1,0:T(8,128)(2,1)}, bf16[256,512]{1,0:T(8,128)(2,1)}, bf16[256,512]{1,0:T(8,128)(2,1)}) custom-call(s32[2,4]{1,0:T(2,128)} %bitcast.1, s32[8,10]{1,0:T(8,128)} %pat_ref.1, bf16[256,4096]{1,0:T(8,128)(2,1)} %q_hbm.1, bf16[256,512]{1,0:T(8,128)(2,1)} %k_hbm.1, bf16[256,512]{1,0:T(8,128)(2,1)} %v_hbm.1, ...), custom_call_target="tpu_custom_call" | custom-call | flops 14495514624 | bytes 9437184 | tf_op jit(solution)/shard_map/pallas_call | solution.py:587
  46.5 4.1 %shard_map.94 = (bf16[256,4096]{1,0:T(8,128)(2,1)}, bf16[256,4096]{1,0:T(8,128)(2,1)}, bf16[256,512]{1,0:T(8,128)(2,1)}, bf16[256,512]{1,0:T(8,128)(2,1)}) custom-call(bf16[256,4096]{1,0:T(8,128)(2,1)} %get-tuple-element.8.refs_0_, bf16[256,4096]{1,0:T(8,128)(2,1)} %get-tuple-element.9.refs_1_, bf16[256,512]{1,0:T(8,128)(2,1)} %get-tuple-element.10.refs_2_, ...), custom_call_target="tpu_custom_call" | custom-call | tf_op jit(solution)/shard_map/pallas_call | solution.py:602
